TPU v7x, 32 devices: a whole 2x2x4 slice. The times are simulated.
32 devices in a mesh: dp: 8 (over z, y), head: 4 (over x, core).
Axes of the slice: x: 2, y: 2, z: 4, core: 2. Of those that a mesh axis runs over, the one named last changes fastest.
Arguments:
- inputs: bfloat16 [16384, 1024], P(('dp', 'head')), may hold values from -6 to 6
- memory: bfloat16 [32, 512, 1024], P('dp'), may hold values from -6 to 6
- compressed: bfloat16 [32, 512, 1024], P('dp'), may hold values from -6 to 6
- slot_valid: int32 [32, 512], P('dp'), may hold values 0 or 1
- slot_age: int32 [32, 512], P('dp'), may hold values from 513 to 3584
- w_query: bfloat16 [1024, 1024], P('dp', 'head'), may hold values from -0.1875 to 0.1875
- w_key: bfloat16 [1024, 1024], P('dp', 'head'), may hold values from -0.1875 to 0.1875
- w_value: bfloat16 [1024, 1024], P('dp', 'head'), may hold values from -0.1875 to 0.1875
- content_bias: bfloat16 [1024], P(('dp', 'head')), may hold values from -3 to 3
- w_out: bfloat16 [1024, 1024], P(('dp', 'head')), may hold values from -2 to 2
- ln_gain: bfloat16 [1024], P(('dp', 'head')), may hold values from 0.5 to 1.5
- ln_bias: bfloat16 [1024], P(('dp', 'head')), may hold values from -2 to 2
- w_up: bfloat16 [1024, 4096], P('dp', 'head'), may hold values from -0.1875 to 0.1875
- up_bias: bfloat16 [4096], P(('dp', 'head')), may hold values from -3 to 3
- w_down: bfloat16 [4096, 1024], P('head', 'dp'), may hold values from -0.09375 to 0.09375
- down_bias: bfloat16 [1024], P(('dp', 'head')), may hold values from -3 to 3
- w_comp: bfloat16 [3, 1024, 1024], P(None, 'dp', 'head'), may hold values from -0.109375 to 0.109375
- comp_bias: bfloat16 [1024], P('head'), may hold values from -3 to 3
- cotangent: bfloat16 [16384, 1024], P(('dp', 'head')), may hold values from -6 to 6
Outputs:
- output: bfloat16 [16384, 1024], P(('dp', 'head'))
- grad_input: float32 [16384, 1024], P(('dp', 'head'))
- grad_query: float32 [1024, 1024], P('dp', 'head')
- grad_key: float32 [1024, 1024], P('dp', 'head')
- grad_value: float32 [1024, 1024], P('dp', 'head')
- grad_content_bias: float32 [1024], P(('dp', 'head'))
- grad_out: float32 [1024, 1024], P(('dp', 'head'))
- grad_ln_gain: float32 [1024], P(('dp', 'head'))
- grad_ln_bias: float32 [1024], P(('dp', 'head'))
- grad_up: float32 [1024, 4096], P('dp', 'head')
- grad_up_bias: float32 [4096], P(('dp', 'head'))
- grad_down: float32 [4096, 1024], P('head', 'dp')
- grad_down_bias: float32 [1024], P(('dp', 'head'))
- new_memory: bfloat16 [32, 512, 1024], P('dp')
- new_compressed: bfloat16 [32, 512, 1024], P('dp', None, 'head')
All inputs are finite; a program needn't handle non-finite values. No bound on the sum of `slot_valid` on one device may be relied on, other than what follows from the above.
Results may differ from a plain program's by a relative error of at most 0.017.
Values may be sent and summed in bfloat16 or wider, within the bound.
No kernel may reach another device: no remote copies, remote signals or barrier semaphores. Data moves between devices by JAX's collectives and lax.ppermute only.
A program may use at most 192 MiB of HBM per device.

v0:
```python
import jax
import jax.numpy as jnp
from jax import lax
from jax.sharding import PartitionSpec as P

D = 1024
HD = 128
SEG = 512
CM = 512
RATE = 3
CC = 171


layer_eps = 1e-05


def head_slopes(first, number):
    return 0.6 * jnp.power(0.7, (first + jnp.arange(number)).astype(jnp.float32))


def score_terms(slopes, slot_mask, slot_dist):
    row_index = jnp.arange(SEG, dtype=jnp.int32)[:, None]
    col_index = jnp.arange(SEG, dtype=jnp.int32)[None, :]
    distance = jnp.concatenate(
        [row_index + slot_dist[None, :], row_index + SEG - col_index, row_index - col_index], axis=1
    )
    allowed = jnp.concatenate(
        [
            jnp.broadcast_to(slot_mask[None, :] > 0, (SEG, CM)),
            jnp.ones((SEG, SEG), dtype=jnp.bool_),
            row_index >= col_index,
        ],
        axis=1,
    )
    log_decay = jnp.log1p(jnp.maximum(distance, 0).astype(jnp.float32))
    return (-slopes[:, None, None] * log_decay[None], allowed)


def seq_scores(queries, key_part, slopes, slot_mask, slot_dist):
    content = jnp.einsum("ihd,jhd->hij", queries, key_part, preferred_element_type=jnp.float32)
    pos_bias, allowed = score_terms(slopes, slot_mask, slot_dist)
    inv_root = queries.shape[-1] ** (-0.5)
    return jnp.where(allowed[None], content * inv_root + pos_bias, -1e30)


def seq_forward(pieces, slopes):
    queries, key_part, value_part, slot_mask, slot_dist = pieces
    scores = seq_scores(queries, key_part, slopes, slot_mask, slot_dist)
    row_max = jnp.max(scores, axis=-1, keepdims=True)
    log_total = row_max + jnp.log(jnp.sum(jnp.exp(scores - row_max), axis=-1, keepdims=True))
    attn_probs = jnp.exp(scores - log_total).astype(jnp.bfloat16)
    mixed_out = jnp.einsum(
        "hij,jhd->ihd", attn_probs, value_part, preferred_element_type=jnp.float32
    )
    return (mixed_out, log_total)


def seq_backward(pieces, slopes):
    queries, key_part, value_part, slot_mask, slot_dist, log_total, grad_out = pieces
    scores = seq_scores(queries, key_part, slopes, slot_mask, slot_dist)
    probs_full = jnp.exp(scores - log_total)
    grad_probs = jnp.einsum(
        "ihd,jhd->hij", grad_out, value_part, preferred_element_type=jnp.float32
    )
    row_dot = jnp.sum(probs_full * grad_probs, axis=-1, keepdims=True)
    grad_scores = (probs_full * (grad_probs - row_dot)).astype(jnp.bfloat16)
    inv_root = queries.shape[-1] ** (-0.5)
    grad_queries = (
        jnp.einsum("hij,jhd->ihd", grad_scores, key_part, preferred_element_type=jnp.float32)
        * inv_root
    )
    grad_keys = (
        jnp.einsum("hij,ihd->jhd", grad_scores, queries, preferred_element_type=jnp.float32)
        * inv_root
    )
    grad_values = jnp.einsum(
        "hij,ihd->jhd",
        probs_full.astype(jnp.bfloat16),
        grad_out,
        preferred_element_type=jnp.float32,
    )
    return (
        grad_queries.astype(jnp.bfloat16),
        grad_keys.astype(jnp.bfloat16),
        grad_values.astype(jnp.bfloat16),
    )


def layer_norm(residual, gain, shift):
    center = residual - jnp.mean(residual, axis=-1, keepdims=True)
    return (
        center * lax.rsqrt(jnp.mean(center * center, axis=-1, keepdims=True) + layer_eps) * gain
        + shift
    )


def per_device(
    inputs,
    memory,
    compressed,
    slot_valid,
    slot_age,
    w_query,
    w_key,
    w_value,
    content_bias,
    w_out,
    ln_gain,
    ln_bias,
    w_up,
    up_bias,
    w_down,
    down_bias,
    w_comp,
    comp_bias,
    cotangent,
):
    member = lax.axis_index("head")
    seq_count = memory.shape[0]
    group_rows = lax.all_gather(inputs, "head", axis=0, tiled=True)
    new_memory = group_rows.reshape(seq_count, SEG, D)
    up_section, down_section = (
        lax.all_gather(w_up, "head", axis=1, tiled=True),
        lax.all_gather(w_down, "head", axis=0, tiled=True),
    )
    query_weight, key_weight, value_weight, squeeze_weight, up_weight, down_weight = (
        lax.all_gather(w_query, "dp", axis=0, tiled=True),
        lax.all_gather(w_key, "dp", axis=0, tiled=True),
        lax.all_gather(w_value, "dp", axis=0, tiled=True),
        lax.all_gather(w_comp, "dp", axis=1, tiled=True),
        lax.all_gather(up_section, "dp", axis=0, tiled=True),
        lax.all_gather(down_section, "dp", axis=1, tiled=True),
    )
    out_weight, bias_query, norm_gain, norm_shift, up_shift, down_shift = (
        lax.all_gather(w_out, ("dp", "head"), axis=0, tiled=True),
        lax.all_gather(content_bias, ("dp", "head"), axis=0, tiled=True),
        lax.all_gather(ln_gain, ("dp", "head"), axis=0, tiled=True),
        lax.all_gather(ln_bias, ("dp", "head"), axis=0, tiled=True),
        lax.all_gather(up_bias, ("dp", "head"), axis=0, tiled=True),
        lax.all_gather(down_bias, ("dp", "head"), axis=0, tiled=True),
    )
    norm_gain = norm_gain.astype(jnp.float32)
    norm_shift = norm_shift.astype(jnp.float32)
    up_shift = up_shift.astype(jnp.float32)
    down_shift = down_shift.astype(jnp.float32)
    col_width = squeeze_weight.shape[2]
    pad_rows = CC * RATE - SEG
    padded = jnp.pad(memory, ((0, 0), (0, pad_rows), (0, 0))).reshape(seq_count, CC, RATE * D)
    squeezed = jnp.dot(
        padded, squeeze_weight.reshape(RATE * D, col_width), preferred_element_type=jnp.float32
    )
    squeezed = squeezed + comp_bias.astype(jnp.float32)
    kept_slots = lax.dynamic_slice_in_dim(compressed[:, CC:, :], member * col_width, col_width, 2)
    new_compressed = jnp.concatenate([kept_slots, squeezed.astype(jnp.bfloat16)], axis=1)
    head_width = query_weight.shape[1]
    local_heads = head_width // HD
    slopes = head_slopes(member * local_heads, local_heads)
    bias_local = lax.dynamic_slice_in_dim(bias_query, member * head_width, head_width).astype(
        jnp.float32
    )
    queries = (
        jnp.dot(group_rows, query_weight, preferred_element_type=jnp.float32) + bias_local
    ).astype(jnp.bfloat16)
    sources = jnp.concatenate([compressed, memory, new_memory], axis=1)
    key_count = sources.shape[1]
    flat_sources = sources.reshape(seq_count * key_count, D)
    key_rows = jnp.dot(flat_sources, key_weight, preferred_element_type=jnp.float32).astype(
        jnp.bfloat16
    )
    value_rows = jnp.dot(flat_sources, value_weight, preferred_element_type=jnp.float32).astype(
        jnp.bfloat16
    )
    query_shape = (seq_count, SEG, local_heads, HD)
    key_shape = (seq_count, key_count, local_heads, HD)
    query_blocks = queries.reshape(query_shape)
    key_blocks = key_rows.reshape(key_shape)
    value_blocks = value_rows.reshape(key_shape)

    def forward_seq(pieces):
        return seq_forward(pieces, slopes)

    mixed_out, log_total = lax.map(
        forward_seq, (query_blocks, key_blocks, value_blocks, slot_valid, slot_age)
    )
    mixed_heads = mixed_out.reshape(seq_count * SEG, head_width).astype(jnp.bfloat16)
    mixed_rows = lax.all_to_all(mixed_heads, "head", split_axis=0, concat_axis=1, tiled=True)
    attn_out = jnp.dot(mixed_rows, out_weight, preferred_element_type=jnp.float32)
    residual = inputs.astype(jnp.float32) + attn_out
    normed, norm_pull = jax.vjp(layer_norm, residual, norm_gain, norm_shift)
    normed_low = normed.astype(jnp.bfloat16)
    before = jnp.dot(normed_low, up_weight, preferred_element_type=jnp.float32) + up_shift
    hidden, gelu_pull = jax.vjp(jax.nn.gelu, before)
    hidden_low = hidden.astype(jnp.bfloat16)
    branch_term = jnp.dot(hidden_low, down_weight, preferred_element_type=jnp.float32)
    output = (residual + branch_term + down_shift).astype(jnp.bfloat16)
    grad_hidden = jnp.dot(cotangent, down_weight.T, preferred_element_type=jnp.float32)
    grad_before = gelu_pull(grad_hidden)[0].astype(jnp.bfloat16)
    grad_down_w = jnp.dot(hidden_low.T, cotangent, preferred_element_type=jnp.float32)
    grad_up_w = jnp.dot(normed_low.T, grad_before, preferred_element_type=jnp.float32)
    up_grad_part = jnp.sum(grad_before.astype(jnp.float32), axis=0)
    normed_term = jnp.dot(grad_before, up_weight.T, preferred_element_type=jnp.float32)
    grad_from_norm, grad_gain, grad_shift = norm_pull(normed_term)
    upstream = cotangent.astype(jnp.float32)
    grad_residual = upstream + grad_from_norm
    grad_down_shift = jnp.sum(upstream, axis=0)
    attn_grad = grad_residual.astype(jnp.bfloat16)
    grad_out_w = jnp.dot(mixed_rows.T, attn_grad, preferred_element_type=jnp.float32)
    grad_mixed = jnp.dot(attn_grad, out_weight.T, preferred_element_type=jnp.float32).astype(
        jnp.bfloat16
    )
    grad_heads = lax.all_to_all(grad_mixed, "head", split_axis=1, concat_axis=0, tiled=True)

    def backward_seq(pieces):
        return seq_backward(pieces, slopes)

    grad_query_all, grad_key_all, grad_value_all = lax.map(
        backward_seq,
        (
            query_blocks,
            key_blocks,
            value_blocks,
            slot_valid,
            slot_age,
            log_total,
            grad_heads.reshape(query_shape),
        ),
    )
    grad_query_rows = grad_query_all.reshape(seq_count * SEG, head_width)
    grad_key_rows = grad_key_all.reshape(seq_count * key_count, head_width)
    grad_value_rows = grad_value_all.reshape(seq_count * key_count, head_width)
    grad_query_w = jnp.dot(group_rows.T, grad_query_rows, preferred_element_type=jnp.float32)
    grad_key_w = jnp.dot(flat_sources.T, grad_key_rows, preferred_element_type=jnp.float32)
    grad_value_w = jnp.dot(flat_sources.T, grad_value_rows, preferred_element_type=jnp.float32)
    bias_grad_part = jnp.sum(grad_query_rows.astype(jnp.float32), axis=0)
    grad_bias_query = lax.dynamic_update_slice_in_dim(
        jnp.zeros((D,), jnp.float32), bias_grad_part, member * head_width, 0
    )
    key_current = grad_key_all[:, CM + SEG :].reshape(seq_count * SEG, head_width)
    value_current = grad_value_all[:, CM + SEG :].reshape(seq_count * SEG, head_width)
    token_term = jnp.dot(grad_query_rows, query_weight.T, preferred_element_type=jnp.float32)
    token_term = token_term + jnp.dot(key_current, key_weight.T, preferred_element_type=jnp.float32)
    token_term = token_term + jnp.dot(
        value_current, value_weight.T, preferred_element_type=jnp.float32
    )
    grad_input = grad_residual + lax.psum_scatter(
        token_term.astype(jnp.bfloat16), "head", scatter_dimension=0, tiled=True
    ).astype(jnp.float32)
    grad_query, grad_key, grad_value, grad_up, grad_down = (
        lax.psum_scatter(
            grad_query_w.astype(jnp.bfloat16), "dp", scatter_dimension=0, tiled=True
        ).astype(jnp.float32),
        lax.psum_scatter(
            grad_key_w.astype(jnp.bfloat16), "dp", scatter_dimension=0, tiled=True
        ).astype(jnp.float32),
        lax.psum_scatter(
            grad_value_w.astype(jnp.bfloat16), "dp", scatter_dimension=0, tiled=True
        ).astype(jnp.float32),
        lax.psum_scatter(
            grad_up_w.astype(jnp.bfloat16), "dp", scatter_dimension=0, tiled=True
        ).astype(jnp.float32),
        lax.psum_scatter(
            grad_down_w.astype(jnp.bfloat16), "dp", scatter_dimension=1, tiled=True
        ).astype(jnp.float32),
    )
    grad_up, grad_down = (
        lax.psum_scatter(
            grad_up.astype(jnp.bfloat16), "head", scatter_dimension=1, tiled=True
        ).astype(jnp.float32),
        lax.psum_scatter(
            grad_down.astype(jnp.bfloat16), "head", scatter_dimension=0, tiled=True
        ).astype(jnp.float32),
    )
    summed_small = (
        lax.psum_scatter(grad_out_w, ("dp", "head"), scatter_dimension=0, tiled=True),
        lax.psum_scatter(grad_bias_query, ("dp", "head"), scatter_dimension=0, tiled=True),
        lax.psum_scatter(grad_gain, ("dp", "head"), scatter_dimension=0, tiled=True),
        lax.psum_scatter(grad_shift, ("dp", "head"), scatter_dimension=0, tiled=True),
        lax.psum_scatter(up_grad_part, ("dp", "head"), scatter_dimension=0, tiled=True),
        lax.psum_scatter(grad_down_shift, ("dp", "head"), scatter_dimension=0, tiled=True),
    )
    return (
        output,
        grad_input,
        grad_query,
        grad_key,
        grad_value,
        summed_small[1],
        summed_small[0],
        summed_small[2],
        summed_small[3],
        grad_up,
        summed_small[4],
        grad_down,
        summed_small[5],
        new_memory,
        new_compressed,
    )


def solution(mesh):
    in_specs = (
        P(("dp", "head"), None),
        P("dp", None, None),
        P("dp", None, None),
        P("dp", None),
        P("dp", None),
        P("dp", "head"),
        P("dp", "head"),
        P("dp", "head"),
        P(("dp", "head")),
        P(("dp", "head"), None),
        P(("dp", "head")),
        P(("dp", "head")),
        P("dp", "head"),
        P(("dp", "head")),
        P("head", "dp"),
        P(("dp", "head")),
        P(None, "dp", "head"),
        P("head"),
        P(("dp", "head"), None),
    )
    out_specs = (
        P(("dp", "head"), None),
        P(("dp", "head"), None),
        P("dp", "head"),
        P("dp", "head"),
        P("dp", "head"),
        P(("dp", "head")),
        P(("dp", "head"), None),
        P(("dp", "head")),
        P(("dp", "head")),
        P("dp", "head"),
        P(("dp", "head")),
        P("head", "dp"),
        P(("dp", "head")),
        P("dp", None, None),
        P("dp", None, "head"),
    )
    return jax.shard_map(
        per_device, mesh=mesh, in_specs=in_specs, out_specs=out_specs, check_vma=False
    )
```

profile of v0, /device:TPU:0, one launch (start us, length us, event | category | flops | bytes accessed | tf_op | source)
XLA Modules:
  0.0 1217.2 jit_solution(385274015754073235)
XLA Ops:
  10.0 19.0 %all-gather.13.cloned.1.call-done = bf16[128,4096]{1,0:T(8,128)(2,1)} async-done(((bf16[128,1024]{1,0:T(8,128)(2,1)}), bf16[128,4096]{1,0:T(8,128)(2,1)}) %all-gather.13.cloned.1.call-update) | async-done | bytes 1048592 | tf_op jit(solution)/shard_map/all_gather | solution.py:123
  32.5 39.8 %all-reduce.11 = (bf16[1024]{0:T(1024)(128)(2,1)S(1)}, bf16[1024]{0:T(1024)(128)(2,1)S(1)}, bf16[1024]{0:T(1024)(128)(2,1)S(1)}, bf16[1024]{0:T(1024)(128)(2,1)}) all-reduce(bf16[1024]{0:T(1024)(128)(2,1)S(1)} %dynamic-update-slice, bf16[1024]{0:T(1024)(128)(2,1)S(1)} %dynamic-update-slice.2, ...), channel_id=1, replica_groups=mesh['dp'=8,'head'=4] {'dp','head'}, use_global_device_ids=true, to_apply=%add.1 | all-reduce | flops 4096 | bytes 16384
  72.3 33.7 %all_gather.46 = bf16[1024,256]{1,0:T(8,128)(2,1)} all-gather(bf16[128,256]{1,0:T(8,128)(2,1)} %param.30), channel_id=1, replica_groups=mesh['dp'=8,'head'=4] {'dp'}, dimensions={0}, use_global_device_ids=true | all-gather | bytes 589824 | tf_op jit(solution)/shard_map/all_gather | solution.py:129
  106.1 34.1 %all_gather.47 = bf16[1024,256]{1,0:T(8,128)(2,1)} all-gather(bf16[128,256]{1,0:T(8,128)(2,1)} %param.28), channel_id=1, replica_groups=mesh['dp'=8,'head'=4] {'dp'}, dimensions={0}, use_global_device_ids=true | all-gather | bytes 589824 | tf_op jit(solution)/shard_map/all_gather | solution.py:127
  140.2 34.8 %all_gather.49 = bf16[1024,256]{1,0:T(8,128)(2,1)} all-gather(bf16[128,256]{1,0:T(8,128)(2,1)} %param.29), channel_id=1, replica_groups=mesh['dp'=8,'head'=4] {'dp'}, dimensions={0}, use_global_device_ids=true | all-gather | bytes 589824 | tf_op jit(solution)/shard_map/all_gather | solution.py:128
  218.3 64.9 %while.32 = (s32[]{:T(128)}, bf16[4,512,2,128]{1,3,2,0:T(8,128)(2,1)}, f32[4,2,512,1]{2,1,3,0:T(2,128)S(1)}, bf16[4,1536,2,128]{3,2,1,0:T(2,128)(2,1)}, s32[4,51...) while((s32[]{:T(128)}, ...), condition=%wide.region_3.4_spmd.clone, body=%wide.region_0.3_spmd.clone.sunk | while | flops 824444416 | bytes 64277168 | solution.py:182
  286.8 47.2 %all-gather = bf16[32,1,128]{2,1,0:T(2,128)(2,1)S(1)} all-gather(bf16[1,1,128]{2,1,0:T(2,128)(2,1)S(1)} %bitcast.222), channel_id=1, replica_groups=mesh['dp'=8,'head'=4] {'dp','head'}, dimensions={0}, use_global_device_ids=true | all-gather | bytes 8448 | tf_op jit(solution)/shard_map/all_gather | solution.py:139
  339.5 12.1 fusion.87
  351.5 46.4 %all-gather.19.cloned.1.call-done = bf16[4096,1024]{1,0:T(8,128)(2,1)} async-done(((bf16[4096,128]{1,0:T(8,128)(2,1)}), bf16[4096,1024]{1,0:T(8,128)(2,1)}) %all-gather.19.cloned.1.call-update) | async-done | bytes 8388624 | tf_op jit(solution)/shard_map/all_gather | solution.py:132
  397.9 14.0 %convert_reduce_fusion = (f32[4096]{0:T(1024)}, bf16[512,4096]{1,0:T(8,128)(2,1)S(1)}) fusion(f32[512,4096]{1,0:T(8,128)} %fusion.87, f32[4096]{0:T(1024)S(1)} %bitcast.219, bf16[512,1024]{1,0:T(8,128)(2,1)S(1)} %copy-done.10, bf16[4096,1024]{1,0:T(8,128)(2,1)} %all-gather.19.cloned.1.call-done), kind=kOutput, calls=%fused_computation.92 | convolution fusion | flops 4343197696 | bytes 22052864 | tf_op jit(solution)/shard_map/dot_general | solution.py:196
  421.5 13.0 %convolution_convert_fusion.2 = bf16[4096,1024]{1,0:T(8,128)(2,1)} fusion(bf16[512,1024]{1,0:T(8,128)(2,1)S(1)} %copy-done.10, f32[512,4096]{1,0:T(8,128)} %fusion.87, f32[4096]{0:T(1024)S(1)} %bitcast.220), kind=kOutput, calls=%fused_computation.97 | convolution fusion | flops 4320133120 | bytes 17842176 | tf_op jit(solution)/shard_map/dot_general | solution.py:198
  434.5 11.9 copy.84
  446.4 11.1 multiply_reduce_fusion.1
  467.9 13.6 %all-to-all-done.1 = bf16[512,4,256]{0,2,1:T(8,128)(2,1)S(1)} async-done(((bf16[512,4,256]{0,2,1:T(8,128)(2,1)}), bf16[512,4,256]{0,2,1:T(8,128)(2,1)S(1)}, u32[]{:S(2)}, u32[]{:S(2)}) %all-to-all-start.1) | async-done | bytes 1048608 | tf_op jit(solution)/shard_map/all_to_all | solution.py:211
  481.5 68.0 %while.33 = (s32[]{:T(128)}, bf16[4,512,2,128]{1,3,2,0:T(8,128)(2,1)}, bf16[4,1536,2,128]{1,3,2,0:T(8,128)(2,1)}, bf16[4,1536,2,128]{1,3,2,0:T(8,128)(2,1)}, bf1...) while((s32[]{:T(128)}, ...), condition=%wide.region_10.11_spmd.clone, body=%wide.region_8.10_spmd.clone.sunk | while | flops 2036991488 | bytes 77113056 | solution.py:216
  615.9 105.0 %reduce-scatter.30.cloned.1.call-done = bf16[128,4096]{1,0:T(8,128)(2,1)} async-done(((bf16[1024,4096]{1,0:T(8,128)(2,1)}), bf16[128,4096]{1,0:T(8,128)(2,1)}) %reduce-scatter.30.cloned.1.call-update) | async-done | bytes 1048592
  740.2 26.1 %all-gather.21.cloned.1.call-done = bf16[3,1024,256]{2,1,0:T(8,128)(2,1)} async-done(((bf16[3,128,256]{2,1,0:T(8,128)(2,1)}), bf16[3,1024,256]{2,1,0:T(8,128)(2,1)}) %all-gather.21.cloned.1.call-update) | async-done | bytes 1572880 | tf_op jit(solution)/shard_map/all_gather | solution.py:130
  771.6 12.4 %add_convert_fusion.1 = bf16[512,1024]{1,0:T(8,128)(2,1)} fusion(f32[512,1024]{1,0:T(8,128)S(1)} %copy-done.6, bf16[4096,1024]{1,0:T(8,128)(2,1)} %all-gather.19.cloned.1.call-done, f32[1024]{0:T(1024)S(1)} %convert_element_type.191, f32[512,4096]{1,0:T(8,128)} %fusion.87, f32[4096]{0:T(1024)S(1)} %bitcast.221), kind=kOutput, calls=%fused_computation.114 | convolution fusion | flops 4317511680 | bytes 19943424 | tf_op jit(solution)/shard_map/dot_general | solution.py:194
  784.4 46.5 %reduce-scatter.28.cloned.1.call-done = bf16[128,256]{1,0:T(8,128)(2,1)} async-done(((bf16[1024,256]{1,0:T(8,128)(2,1)}), bf16[128,256]{1,0:T(8,128)(2,1)}) %reduce-scatter.28.cloned.1.call-update) | async-done | bytes 65552
  832.6 63.5 %reduce-scatter.16.cloned.1.call-done = bf16[128,256]{1,0:T(8,128)(2,1)} async-done(((bf16[1024,256]{1,0:T(8,128)(2,1)}), bf16[128,256]{1,0:T(8,128)(2,1)}) %reduce-scatter.16.cloned.1.call-update) | async-done | bytes 65552 | tf_op jit(solution)/shard_map/reduce_scatter | solution.py:252
  897.6 62.7 %reduce-scatter.18.cloned.1.call-done = bf16[128,256]{1,0:T(8,128)(2,1)} async-done(((bf16[1024,256]{1,0:T(8,128)(2,1)}), bf16[128,256]{1,0:T(8,128)(2,1)}) %reduce-scatter.18.cloned.1.call-update) | async-done | bytes 65552 | tf_op jit(solution)/shard_map/reduce_scatter | solution.py:255
  961.8 45.3 %reduce-scatter.14.cloned.1.call-done = bf16[512,1024]{1,0:T(8,128)(2,1)} async-done(((bf16[2048,1024]{1,0:T(8,128)(2,1)}), bf16[512,1024]{1,0:T(8,128)(2,1)}) %reduce-scatter.14.cloned.1.call-update) | async-done | bytes 1048592 | tf_op jit(solution)/shard_map/reduce_scatter | solution.py:245
  1010.1 39.8 %all-reduce.10 = (f32[1024]{0:T(1024)S(1)}, f32[1024]{0:T(1024)S(1)}, f32[1024]{0:T(1024)S(1)}, f32[4096]{0:T(1024)S(1)}, f32[1024]{0:T(1024)S(1)}) all-reduce(f32[1024]{0:T(1024)S(1)} %bitcast_dynamic-update-slice_fusion.1, f32[1024]{0:T(1024)S(1)} %copy-done.31, ...), channel_id=6, replica_groups=mesh['dp'=8,'head'=4] {'dp','head'}, use_global_device_ids=true, to_apply=%region_16.17.clone | all-reduce | flops 8192 | bytes 65536
  1063.6 142.0 %reduce-scatter.20.cloned.1.call-done = f32[32,1024]{1,0:T(8,128)} async-done(((f32[1024,1024]{1,0:T(8,128)}), f32[32,1024]{1,0:T(8,128)}) %reduce-scatter.20.cloned.1.call-update) | async-done | bytes 131088 | tf_op jit(solution)/shard_map/reduce_scatter | solution.py:274
  (355 shorter events, 327.2 us)
Async XLA Ops:
  7.2 21.9 %all-gather.13.cloned.1.call-start = ((), (), s32[]{:S(2)}) async-start(), calls=%async_computation.13 | async-start | bytes 1310720 | tf_op jit(solution)/shard_map/all_gather | solution.py:123
  7.9 167.1 %all-gather.17.cloned.1.call-start = ((), (), s32[]{:S(2)}) async-start(), calls=%async_computation.15 | async-start | bytes 1310720 | tf_op jit(solution)/shard_map/all_gather | solution.py:124
  8.7 166.4 %all-gather.9.cloned.1.call-start = ((), (), s32[]{:S(2)}) async-start(), calls=%async_computation.11 | async-start | bytes 5242880 | tf_op jit(solution)/shard_map/all_gather | solution.py:120
  9.4 324.7 %all-gather.11.cloned.1.call-start = ((), (), s32[]{:S(2)}) async-start(), calls=%async_computation.12 | async-start | bytes 2162688 | tf_op jit(solution)/shard_map/all_gather | solution.py:135
  10.0 329.5 %all-gather.15.cloned.1.call-start = ((), (), s32[]{:S(2)}) async-start(), calls=%async_computation.14 | async-start | bytes 9437184 | tf_op jit(solution)/shard_map/all_gather | solution.py:131
  29.1 368.9 %all-gather.19.cloned.1.call-start = ((), (), s32[]{:S(2)}) async-start(), calls=%async_computation.16 | async-start | bytes 9437184 | tf_op jit(solution)/shard_map/all_gather | solution.py:132
  283.2 50.9 %all-to-all-start = ((bf16[4,512,256]{1,2,0:T(8,128)(2,1)}), bf16[4,512,256]{1,2,0:T(8,128)(2,1)S(1)}, u32[]{:S(2)}, u32[]{:S(2)}) async-start(bf16[4,512,256]{1,2,0:T(8,128)(2,1)} %bitcast.216), calls=%async_computation | async-start | bytes 2097152 | tf_op jit(solution)/shard_map/all_to_all | solution.py:186
  286.8 328.6 %reduce-scatter.22.cloned.1.call-start = ((), (), s32[]{:S(2)}) async-start(), calls=%async_computation.21 | async-start | bytes 9437184 | tf_op jit(solution)/shard_map/reduce_scatter | solution.py:258
  421.4 299.4 %reduce-scatter.30.cloned.1.call-start = ((), (), s32[]{:S(2)}) async-start(), calls=%async_computation.26 | async-start | bytes 9437184
  463.5 18.0 %all-to-all-start.1 = ((bf16[512,4,256]{0,2,1:T(8,128)(2,1)}), bf16[512,4,256]{0,2,1:T(8,128)(2,1)S(1)}, u32[]{:S(2)}, u32[]{:S(2)}) async-start(bf16[512,4,256]{0,2,1:T(8,128)(2,1)} %bitcast.210), calls=%async_computation.1 | async-start | bytes 2097152 | tf_op jit(solution)/shard_map/all_to_all | solution.py:211
  467.1 299.2 %all-gather.21.cloned.1.call-start = ((), (), s32[]{:S(2)}) async-start(), calls=%async_computation.24 | async-start | bytes 1769472 | tf_op jit(solution)/shard_map/all_gather | solution.py:130
  467.8 363.0 %reduce-scatter.28.cloned.1.call-start = ((), (), s32[]{:S(2)}) async-start(), calls=%async_computation.25 | async-start | bytes 589824
  579.0 317.1 %reduce-scatter.16.cloned.1.call-start = ((), (), s32[]{:S(2)}) async-start(), calls=%async_computation.18 | async-start | bytes 589824 | tf_op jit(solution)/shard_map/reduce_scatter | solution.py:252
  589.1 371.1 %reduce-scatter.18.cloned.1.call-start = ((), (), s32[]{:S(2)}) async-start(), calls=%async_computation.19 | async-start | bytes 589824 | tf_op jit(solution)/shard_map/reduce_scatter | solution.py:255
  599.1 408.0 %reduce-scatter.14.cloned.1.call-start = ((), (), s32[]{:S(2)}) async-start(), calls=%async_computation.17 | async-start | bytes 5242880 | tf_op jit(solution)/shard_map/reduce_scatter | solution.py:245
  615.2 437.6 %reduce-scatter.24.cloned.1.call-start = ((), (), s32[]{:S(2)}) async-start(), calls=%async_computation.22 | async-start | bytes 1310720 | tf_op jit(solution)/shard_map/reduce_scatter | solution.py:266
  615.8 446.0 %reduce-scatter.26.cloned.1.call-start = ((), (), s32[]{:S(2)}) async-start(), calls=%async_computation.23 | async-start | bytes 1310720 | tf_op jit(solution)/shard_map/reduce_scatter | solution.py:269
  723.1 482.5 %reduce-scatter.20.cloned.1.call-start = ((), (), s32[]{:S(2)}) async-start(), calls=%async_computation.20 | async-start | bytes 4325376 | tf_op jit(solution)/shard_map/reduce_scatter | solution.py:274
  771.5 235.6 %copy-start.2 = (f32[512,1024]{1,0:T(8,128)S(1)}, f32[512,1024]{1,0:T(8,128)}, u32[]{:S(2)}) copy-start(f32[512,1024]{1,0:T(8,128)} %copy-done.1) | copy-start | bytes 6291460
  771.5 235.5 %copy-start.11 = (bf16[512,1024]{1,0:T(8,128)(2,1)S(1)}, bf16[512,1024]{1,0:T(8,128)(2,1)}, u32[]{:S(2)}) copy-start(bf16[512,1024]{1,0:T(8,128)(2,1)} %param.41) | copy-start | bytes 3145732
  771.6 235.5 %copy-start.27 = (f32[512]{0:T(512)S(1)}, f32[512]{0:T(512)}, u32[]{:S(2)}) copy-start(f32[512]{0:T(512)} %copy-done.26) | copy-start | bytes 6148
  784.0 226.1 %copy-start.28 = (f32[4096]{0:T(1024)S(1)}, f32[4096]{0:T(1024)}, u32[]{:S(2)}) copy-start(f32[4096]{0:T(1024)} %get-tuple-element.478) | copy-start | bytes 49156
  784.0 226.1 %copy-start.31 = (f32[1024]{0:T(1024)S(1)}, f32[1024]{0:T(1024)}, u32[]{:S(2)}) copy-start(f32[1024]{0:T(1024)} %get-tuple-element.422) | copy-start | bytes 12292
  784.0 226.1 %copy-start.32 = (f32[1024]{0:T(1024)S(1)}, f32[1024]{0:T(1024)}, u32[]{:S(2)}) copy-start(f32[1024]{0:T(1024)} %get-tuple-element.424) | copy-start | bytes 12292
  (40 other events, 597.8 us)
Sparse Core Ops, SparseCore 0:
  9.6 19.4 all-gather.12
  30.6 17.0 all-gather.16
  49.3 35.0 all-gather.8
  87.1 57.8 all-gather.10
  147.0 125.3 all-gather.14
  274.3 123.5 all-gather.18
  421.6 147.1 reduce-scatter.21
  572.8 148.0 reduce-scatter.29
  723.1 43.1 all-gather.20
  770.0 60.7 reduce-scatter.27
  835.1 60.9 reduce-scatter.15
  899.3 60.9 reduce-scatter.17
  963.5 43.5 reduce-scatter.13
  1009.5 24.8 reduce-scatter.23
  1036.9 24.8 reduce-scatter.25
  1064.5 141.0 reduce-scatter.19
where the time goes:
time: 1230 us; the launch traced here: 1220 us
  waiting for transfers between devices  581 us (47%)
  blocking collectives  229 us (19%)
  matrix products  224 us (18%)
  local copies, waits for them, and re-layouts  116 us (9%)
  other arithmetic  42.1 us (3%)
  between operations  15 us (1%)
    unnamed x18, waiting for transfers between devices  155 us
    reduce_scatter x1, waiting for transfers between devices, per_device(): lax.psum_scatter(grad_out_w, ('dp', 'head'), scatter_dimension=0, tiled=T...  142 us
    unnamed x2, blocking collectives  79.5 us
    reduce_scatter x1, waiting for transfers between devices, per_device(): lax.psum_scatter(grad_key_w.astype(jnp.bfloat16), 'dp', scatter_dimension...  63.5 us
    reduce_scatter x1, waiting for transfers between devices, per_device(): lax.psum_scatter(grad_value_w.astype(jnp.bfloat16), 'dp', scatter_dimensi...  62.7 us
    all_gather x1, blocking collectives, per_device(): lax.all_gather(up_bias, ('dp', 'head'), axis=0, tiled=True)  47.2 us
    all_gather x1, waiting for transfers between devices, per_device(): lax.all_gather(down_section, 'dp', axis=1, tiled=True)  46.4 us
    reduce_scatter x1, waiting for transfers between devices, per_device(): lax.psum_scatter(token_term.astype(jnp.bfloat16), 'head', scatter_dimensi...  45.3 us
  transfers between devices with their start and end apart: 18, of which 11 were waited for; matrix products, arithmetic and copies ran while one was open for 27% of the time, Pallas kernels for 0%

commit v1 on v0

v1 whole, which is shorter than its diff:
```python
import functools

import jax
import jax.numpy as jnp
from jax import lax
from jax.experimental import pallas as pl
from jax.experimental.pallas import tpu as pltpu
from jax.sharding import PartitionSpec as P

D = 1024
HD = 128
SEG = 512
CM = 512
RATE = 3
CC = 171
LN_EPS = 1e-05
LOG2E = 1.4426950408889634
SCALE2 = LOG2E * HD ** (-0.5)
FAR = 1e32
VMEM = 56 * 1024 * 1024
BF = jnp.bfloat16
F32 = jnp.float32


def nt(a, b):
    return lax.dot_general(a, b, (((1,), (1,)), ((), ())), preferred_element_type=F32)


def tn(a, b):
    return lax.dot_general(a, b, (((0,), (0,)), ((), ())), preferred_element_type=F32)


def nn(a, b):
    return jnp.dot(a, b, preferred_element_type=F32)


def x_swap(a):
    return lax.ppermute(a, "head", [(i, i ^ 2) for i in range(4)])


def c_swap(a):
    return lax.ppermute(a, "head", [(i, i ^ 1) for i in range(4)])


def fwd_kernel(slope_ref, q_ref, kv_ref, near_ref, far_ref, mixed_ref, lse_ref):
    a = pl.program_id(0)
    slope2 = slope_ref[a] * LOG2E
    q = q_ref[...]
    parts = []
    for n in range(3):
        k = kv_ref[n * SEG:(n + 1) * SEG, :HD]
        table = far_ref[...] if n == 0 else near_ref[(n - 1) * SEG:n * SEG, :]
        parts.append(nt(k, q) * SCALE2 - slope2 * table)
    top = jnp.maximum(jnp.maximum(jnp.max(parts[0], axis=0, keepdims=True), jnp.max(parts[1], axis=0, keepdims=True)),
                      jnp.max(parts[2], axis=0, keepdims=True))
    total = jnp.zeros((1, SEG), F32)
    acc = jnp.zeros((HD, SEG), F32)
    for n in range(3):
        p = jnp.exp2(parts[n] - top)
        total = total + jnp.sum(p, axis=0, keepdims=True)
        acc = acc + tn(kv_ref[n * SEG:(n + 1) * SEG, HD:], p.astype(BF))
    mixed_ref[...] = (acc / total).T.astype(BF)
    lse_ref[...] = (top + jnp.log2(total)).reshape(1, 1, SEG)


def bwd_kernel(slope_ref, q_ref, kv_ref, near_ref, far_ref, mixed_ref, lse_ref, do_ref, dq_ref, dkv_ref):
    a = pl.program_id(0)
    slope2 = slope_ref[a] * LOG2E
    q = q_ref[...]
    do = do_ref[...]
    lse = lse_ref[...].reshape(1, SEG)
    row_dot = jnp.sum((do.astype(F32) * mixed_ref[...].astype(F32)).T, axis=0, keepdims=True)
    inv_root = HD ** (-0.5)
    dq = jnp.zeros((HD, SEG), F32)
    for n in range(3):
        rows = slice(n * SEG, (n + 1) * SEG)
        k = kv_ref[rows, :HD]
        v = kv_ref[rows, HD:]
        table = far_ref[...] if n == 0 else near_ref[(n - 1) * SEG:n * SEG, :]
        p = jnp.exp2(nt(k, q) * SCALE2 - slope2 * table - lse)
        ds = (p * (nt(v, do) - row_dot)).astype(BF)
        dkv_ref[rows, HD:] = nn(p.astype(BF), do).astype(BF)
        dkv_ref[rows, :HD] = (nn(ds, q) * inv_root).astype(BF)
        dq = dq + tn(k, ds)
    dq_ref[...] = (dq.T * inv_root).astype(BF)


ROWS = 3 * SEG
PARAMS = pltpu.CompilerParams(vmem_limit_bytes=VMEM)
smem_spec = pl.BlockSpec(memory_space=pltpu.SMEM)
q_spec = pl.BlockSpec((SEG, HD), lambda a: (0, a))
kv_spec = pl.BlockSpec((ROWS, 2 * HD), lambda a: (0, a))
near_spec = pl.BlockSpec((2 * SEG, SEG), lambda a: (0, 0))
far_spec = pl.BlockSpec((SEG, SEG), lambda a: (0, 0))
lse_spec = pl.BlockSpec((1, 1, SEG), lambda a: (a, 0, 0))


def attend(slopes, q, kv, near, far):
    return pl.pallas_call(
        fwd_kernel,
        grid=(2,),
        in_specs=[smem_spec, q_spec, kv_spec, near_spec, far_spec],
        out_specs=[q_spec, lse_spec],
        out_shape=[jax.ShapeDtypeStruct((SEG, 2 * HD), BF), jax.ShapeDtypeStruct((2, 1, SEG), F32)],
        compiler_params=PARAMS,
        cost_estimate=pl.CostEstimate(flops=2 * 4 * SEG * ROWS * HD, bytes_accessed=6 << 20, transcendentals=2 * SEG * ROWS),
    )(slopes, q, kv, near, far)


def attend_back(slopes, q, kv, near, far, mixed, lse, do):
    return pl.pallas_call(
        bwd_kernel,
        grid=(2,),
        in_specs=[smem_spec, q_spec, kv_spec, near_spec, far_spec, q_spec, lse_spec, q_spec],
        out_specs=[q_spec, kv_spec],
        out_shape=[jax.ShapeDtypeStruct((SEG, 2 * HD), BF), jax.ShapeDtypeStruct((ROWS, 4 * HD), BF)],
        compiler_params=PARAMS,
        cost_estimate=pl.CostEstimate(flops=2 * 10 * SEG * ROWS * HD, bytes_accessed=8 << 20, transcendentals=2 * SEG * ROWS),
    )(slopes, q, kv, near, far, mixed, lse, do)


def gelu_pair(before):
    c0, c1 = 0.7978845608028654, 0.044715
    sq = before * before
    t = jnp.tanh(c0 * before * (1.0 + c1 * sq))
    half = 0.5 * (1.0 + t)
    return before * half, half + 0.5 * before * (1.0 - t * t) * (c0 * (1.0 + 3.0 * c1 * sq))


def butterfly(a, n_dp):
    a = a + c_swap(a)
    a = a + x_swap(a)
    step = 1
    while step < n_dp:
        a = a + lax.ppermute(a, "dp", [(i, i ^ step) for i in range(n_dp)])
        step *= 2
    return a


def per_device(
    inputs,
    memory,
    compressed,
    slot_valid,
    slot_age,
    w_query,
    w_key,
    w_value,
    content_bias,
    w_out,
    ln_gain,
    ln_bias,
    w_up,
    up_bias,
    w_down,
    down_bias,
    w_comp,
    comp_bias,
    cotangent,
):
    n_dp = lax.axis_size("dp")
    d = lax.axis_index("dp")
    h = lax.axis_index("head")
    seqs = memory.shape[0]
    kw = w_key.shape[0]

    pack = jnp.concatenate(
        [w_key[:, :HD], w_value[:, :HD], w_key[:, HD:], w_value[:, HD:], w_query], axis=1
    )
    w_own = lax.all_gather(pack, "dp", axis=0, tiled=True)
    inputs_x = x_swap(inputs)
    w_par = c_swap(w_own)
    small = jnp.concatenate([content_bias, ln_gain, ln_bias, down_bias, up_bias]).reshape(1, -1)
    small = lax.all_gather(small, ("dp", "head"), axis=0, tiled=True).astype(F32)
    out_rows = w_out.shape[0]
    wo = lax.all_gather(w_out, "dp", axis=0, tiled=True)
    wo2 = jnp.stack([wo, c_swap(wo)])
    wo4 = jnp.concatenate([wo2, x_swap(wo2)]).reshape(4, n_dp, out_rows, D)
    w_o = jnp.take(wo4, h ^ jnp.arange(4), axis=0).transpose(1, 0, 2, 3).reshape(4, D // 4, D)
    w_o = jnp.take(w_o, h ^ jnp.arange(4), axis=0).reshape(D, D)
    cot_x = x_swap(cotangent)
    up_own = lax.all_gather(w_up, "dp", axis=0, tiled=True)
    down_own = lax.all_gather(w_down.T, "dp", axis=0, tiled=True)
    up_par = c_swap(up_own)
    down_par = c_swap(down_own)
    comp_w = lax.all_gather(w_comp, "dp", axis=1, tiled=True)

    other = c_swap(jnp.stack([inputs, inputs_x]))
    four = jnp.concatenate([jnp.stack([inputs, inputs_x]), other])
    rank = jnp.arange(4)
    new_memory = jnp.take(four, ((rank ^ h) >> 1) | (((rank ^ h) & 1) << 1), axis=0)

    share = content_bias.shape[0]
    bias_all = small[:, :share].reshape(4, 2 * HD)
    gain = small[:, share:2 * share].reshape(1, D)
    shift = small[:, 2 * share:3 * share].reshape(1, D)
    down_shift = small[:, 3 * share:4 * share].reshape(1, D)
    up_shift = small[:, 4 * share:].reshape(4, D)

    i = jnp.arange(SEG, dtype=jnp.int32)[None, :]
    j = jnp.arange(2 * SEG, dtype=jnp.int32)[:, None]
    gap = i + SEG - j
    near = jnp.where(gap >= 0, jnp.log1p(jnp.maximum(gap, 0).astype(F32)), FAR)

    def far_of(s):
        age = lax.dynamic_index_in_dim(slot_age, s, 0, keepdims=False)[:, None]
        valid = lax.dynamic_index_in_dim(slot_valid, s, 0, keepdims=False)[:, None]
        return jnp.where(valid > 0, jnp.log1p(jnp.maximum(i + age, 0).astype(F32)), FAR)

    groups = (h, h ^ 1)
    slopes = [0.6 * jnp.power(0.7, (2 * g + jnp.arange(2)).astype(F32)) for g in groups]
    weights = (w_own, w_par)
    seq_ids = (h, h ^ 2)
    tokens = (inputs, inputs_x)
    far = [far_of(s) for s in seq_ids]
    sources = [
        jnp.concatenate(
            [lax.dynamic_index_in_dim(compressed, s, 0, keepdims=False),
             lax.dynamic_index_in_dim(memory, s, 0, keepdims=False), t], axis=0)
        for s, t in zip(seq_ids, tokens)
    ]

    q, kv, mixed, lse = {}, {}, {}, {}
    for t in (1, 0):
        for g in (0, 1):
            bias = lax.dynamic_index_in_dim(bias_all, groups[g], 0, keepdims=True)
            q[t, g] = (nn(tokens[t], weights[g][:, 4 * HD:]) + bias).astype(BF)
            kv[t, g] = nn(sources[t], weights[g][:, :4 * HD]).astype(BF)
            mixed[t, g], lse[t, g] = attend(slopes[g], q[t, g], kv[t, g], near, far[t])
    sent = x_swap(jnp.concatenate([mixed[1, 0], mixed[1, 1]], axis=1))
    mixed_rows = jnp.concatenate([mixed[0, 0], mixed[0, 1], sent], axis=1)
    residual = inputs.astype(F32) + nn(mixed_rows, w_o)
    center = residual - jnp.mean(residual, axis=-1, keepdims=True)
    rstd = lax.rsqrt(jnp.mean(center * center, axis=-1, keepdims=True) + LN_EPS)
    normed = (center * rstd * gain + shift).astype(BF)
    normed_x = x_swap(normed)

    ups, downs = (up_own, up_par), (down_own, down_par)
    norm2, cot2 = (normed, normed_x), (cotangent, cot_x)
    hidden, grad_b, branch, grad_n = {}, {}, {}, {}
    for t in (0, 1):
        for g in (0, 1):
            shift_g = lax.dynamic_index_in_dim(up_shift, groups[g], 0, keepdims=True)
            before = nn(norm2[t], ups[g]) + shift_g
            act, slope = gelu_pair(before)
            hidden[t, g] = act.astype(BF)
            grad_b[t, g] = (nn(cot2[t], downs[g]) * slope).astype(BF)
        grad_n[t] = nt(grad_b[t, 0], ups[0]) + nt(grad_b[t, 1], ups[1])
        branch[t] = nt(hidden[t, 0], downs[0]) + nt(hidden[t, 1], downs[1])
    grad_n_x = x_swap(grad_n[1].astype(BF))
    branch_x = x_swap(branch[1].astype(BF))
    grad_normed = grad_n[0] + grad_n_x.astype(F32)
    output = (residual + branch[0] + branch_x.astype(F32) + down_shift).astype(BF)

    g_up = [tn(normed, grad_b[0, g]) + tn(normed_x, grad_b[1, g]) for g in (0, 1)]
    g_down = [tn(cotangent, hidden[0, g]) + tn(cot_x, hidden[1, g]) for g in (0, 1)]
    g_up_sum = (g_up[0] + c_swap(g_up[1].astype(BF)).astype(F32)).astype(BF)
    g_down_sum = (g_down[0] + c_swap(g_down[1].astype(BF)).astype(F32)).astype(BF)
    grad_up = lax.psum_scatter(g_up_sum, "dp", scatter_dimension=0, tiled=True).astype(F32)
    grad_down = lax.psum_scatter(g_down_sum, "dp", scatter_dimension=0, tiled=True).astype(F32).T
    up_cols = [jnp.sum(grad_b[0, g].astype(F32), axis=0) + jnp.sum(grad_b[1, g].astype(F32), axis=0) for g in (0, 1)]

    xhat = center * rstd
    g = grad_normed * gain
    upstream = cotangent.astype(F32)
    grad_residual = upstream + rstd * (
        g - jnp.mean(g, axis=-1, keepdims=True) - xhat * jnp.mean(g * xhat, axis=-1, keepdims=True)
    )
    attn_grad = grad_residual.astype(BF)
    grad_mixed = nt(attn_grad, w_o).astype(BF)
    half = D // 2
    got = x_swap(grad_mixed[:, half:])
    g_out = tn(mixed_rows, attn_grad).astype(BF).reshape(4, D // 4, D)
    g_out = jnp.take(g_out, h ^ jnp.arange(4), axis=0).reshape(n_dp, 2, 2, out_rows, D)
    cc, xx = h % 2, h // 2
    pick = lambda a, n, axis: lax.dynamic_index_in_dim(a, n, axis, keepdims=False)
    g_out = (pick(g_out, cc, 2).astype(F32) + c_swap(pick(g_out, 1 - cc, 2)).astype(F32)).astype(BF)
    g_out = (pick(g_out, xx, 1).astype(F32) + x_swap(pick(g_out, 1 - xx, 1)).astype(F32)).astype(BF)
    grad_out = lax.psum_scatter(g_out.reshape(n_dp * out_rows, D), "dp", scatter_dimension=0, tiled=True).astype(F32)

    do = {(0, 0): grad_mixed[:, :2 * HD], (0, 1): grad_mixed[:, 2 * HD:half],
          (1, 0): got[:, :2 * HD], (1, 1): got[:, 2 * HD:]}
    dq, dkv = {}, {}
    term = {}
    for t in (0, 1):
        for g in (0, 1):
            dq[t, g], dkv[t, g] = attend_back(
                slopes[g], q[t, g], kv[t, g], near, far[t], mixed[t, g], lse[t, g], do[t, g])
        term[t] = sum(nt(dkv[t, g][2 * SEG:], weights[g][:, :4 * HD]) + nt(dq[t, g], weights[g][:, 4 * HD:]) for g in (0, 1))
    term_x = x_swap(term[1].astype(BF))
    grad_input = grad_residual + term[0] + term_x.astype(F32)
    g_w = []
    for g in (0, 1):
        g_kv = tn(sources[0], dkv[0, g]) + tn(sources[1], dkv[1, g])
        g_q = tn(inputs, dq[0, g]) + tn(inputs_x, dq[1, g])
        g_w.append((g_kv, g_q))
    from_par = c_swap(jnp.concatenate([g_w[1][0].astype(BF), g_w[1][1].astype(BF)], axis=1))
    g_sum = jnp.concatenate(
        [(g_w[0][0] + from_par[:, :4 * HD].astype(F32)).astype(BF),
         (g_w[0][1] + from_par[:, 4 * HD:].astype(F32)).astype(BF)], axis=1)
    g_sum = lax.psum_scatter(g_sum, "dp", scatter_dimension=0, tiled=True).astype(F32)
    grad_key = jnp.concatenate([g_sum[:, :HD], g_sum[:, 2 * HD:3 * HD]], axis=1)
    grad_value = jnp.concatenate([g_sum[:, HD:2 * HD], g_sum[:, 3 * HD:4 * HD]], axis=1)
    grad_query = g_sum[:, 4 * HD:]

    lane = jnp.arange(4)[:, None]
    place = lambda parts: jnp.where(lane == groups[0], parts[0][None], 0.0) + jnp.where(lane == groups[1], parts[1][None], 0.0)
    bias_cols = [jnp.sum(dq[0, g].astype(F32), axis=0) + jnp.sum(dq[1, g].astype(F32), axis=0) for g in (0, 1)]
    early = jnp.concatenate([
        jnp.sum(grad_normed * xhat, axis=0).reshape(-1, share),
        jnp.sum(grad_normed, axis=0).reshape(-1, share),
        jnp.sum(upstream, axis=0).reshape(-1, share),
        place(up_cols).reshape(-1, up_bias.shape[0]),
    ], axis=1)
    early = pick(butterfly(early, n_dp), d * 4 + h, 0)
    late = pick(butterfly(place(bias_cols).reshape(-1, share), n_dp), d * 4 + h, 0)

    width = comp_w.shape[2]
    padded = jnp.pad(memory, ((0, 0), (0, CC * RATE - SEG), (0, 0))).reshape(seqs, CC, RATE * D)
    squeezed = nn(padded, comp_w.reshape(RATE * D, width)) + comp_bias.astype(F32)
    kept = lax.dynamic_slice_in_dim(compressed[:, CC:, :], h * width, width, 2)
    new_compressed = jnp.concatenate([kept, squeezed.astype(BF)], axis=1)

    return (
        output,
        grad_input,
        grad_query,
        grad_key,
        grad_value,
        late,
        grad_out,
        early[:share],
        early[share:2 * share],
        grad_up,
        early[3 * share:],
        grad_down,
        early[2 * share:3 * share],
        new_memory,
        new_compressed,
    )


def solution(mesh):
    both = ("dp", "head")
    in_specs = (
        P(both, None),
        P("dp", None, None),
        P("dp", None, None),
        P("dp", None),
        P("dp", None),
        P("dp", "head"),
        P("dp", "head"),
        P("dp", "head"),
        P(both),
        P(both, None),
        P(both),
        P(both),
        P("dp", "head"),
        P(both),
        P("head", "dp"),
        P(both),
        P(None, "dp", "head"),
        P("head"),
        P(both, None),
    )
    out_specs = (
        P(both, None),
        P(both, None),
        P("dp", "head"),
        P("dp", "head"),
        P("dp", "head"),
        P(both),
        P(both, None),
        P(both),
        P(both),
        P("dp", "head"),
        P(both),
        P("head", "dp"),
        P(both),
        P("dp", None, None),
        P("dp", None, "head"),
    )
    return jax.shard_map(per_device, mesh=mesh, in_specs=in_specs, out_specs=out_specs, check_vma=False)
```

time: 1230 us -> 654 us (0.53)
  waiting for transfers between devices: 581 us -> 215 us
  blocking collectives: 229 us -> 87.9 us
  matrix products: 224 us -> 133 us
  Pallas kernels: 0 us -> 57.5 us
  local copies, waits for them, and re-layouts: 116 us -> 69.1 us
    reduce_scatter x7 -> x2, waiting for transfers between devices: 321 us -> 0.01 us  [the longest x1 0.01 us: per_device(): lax.psum_scatter(g_out.reshape(n_dp * out_rows, D), 'dp', scatter_dimensi...]
    ppermute x0 -> x29, waiting for transfers between devices: none -> 105 us  [the longest x12 87.6 us: x_swap(): return lax.ppermute(a, 'head', [(i, i ^ 2) for i in range(4)])]
    all_gather x7 -> x4, waiting for transfers between devices: 91.6 us -> 0.01 us  [the longest x1 0.01 us: per_device(): w_own = lax.all_gather(pack, 'dp', axis=0, tiled=True)]
    dot_general x47 -> x52, matrix products: 224 us -> 133 us  [the longest x18 52.5 us: nn(): return jnp.dot(a, b, preferred_element_type=F32)]
    unnamed x2 -> x0, blocking collectives: 79.5 us -> none
    all_gather x4 -> x2, blocking collectives: 150 us -> 87.9 us  [the longest x1 55 us: per_device(): lax.all_gather(small, ('dp', 'head'), axis=0, tiled=True).astype(F32)]
    pallas_call x0 -> x8, Pallas kernels: none -> 57.5 us  [the longest x4 32.1 us: attend_back(): pl.pallas_call(bwd_kernel, grid=(2,), in_specs=[smem_spec, q_spec, kv_spe...]
    unnamed x18 -> x10, waiting for transfers between devices: 155 us -> 110 us
  transfers between devices with their start and end apart: 18 -> 37, of which waited for: 11 -> 13; matrix products, arithmetic and copies ran while one was open for 27% -> 34% of each run, Pallas kernels for 0% -> 9%
where the time goes in v1:
time: 654 us; the launch traced here: 649 us
  waiting for transfers between devices  215 us (33%)
  matrix products  133 us (20%)
  blocking collectives  87.9 us (13%)
  local copies, waits for them, and re-layouts  69.1 us (11%)
  Pallas kernels  57.5 us (9%)
  other arithmetic  51.9 us (8%)
  starting transfers between devices  18.8 us (3%)
  between operations  15.6 us (2%)
    unnamed x10, waiting for transfers between devices  110 us
    ppermute x12, waiting for transfers between devices, x_swap(): return lax.ppermute(a, 'head', [(i, i ^ 2) for i in range(4)])  87.6 us
    all_gather x1, blocking collectives, per_device(): lax.all_gather(small, ('dp', 'head'), axis=0, tiled=True).astype(F32)  55 us
    dot_general x18, matrix products, nn(): return jnp.dot(a, b, preferred_element_type=F32)  52.5 us
    dot_general x17, matrix products, tn(): lax.dot_general(a, b, (((0,), (0,)), ((), ())), preferred_element_type=F32)  45.6 us
    dot_general x17, matrix products, nt(): lax.dot_general(a, b, (((1,), (1,)), ((), ())), preferred_element_type=F32)  34.9 us
    all_gather x1, blocking collectives, per_device(): wo = lax.all_gather(w_out, 'dp', axis=0, tiled=True)  32.9 us
    pallas_call x4, Pallas kernels, attend_back(): pl.pallas_call(bwd_kernel, grid=(2,), in_specs=[smem_spec, q_spec, kv_spe...  32.1 us
  transfers between devices with their start and end apart: 37, of which 13 were waited for; matrix products, arithmetic and copies ran while one was open for 34% of the time, Pallas kernels for 9%

profile of v1, /device:TPU:0, one launch (start us, length us, event | category | flops | bytes accessed | tf_op | source)
XLA Modules:
  0.0 648.9 jit_solution(11918004022101856997)
XLA Ops:
  16.4 32.9 %all_gather.20 = bf16[256,1024]{1,0:T(8,128)(2,1)S(1)} all-gather(bf16[32,1024]{1,0:T(8,128)(2,1)} %param.30), channel_id=1, replica_groups=mesh['dp'=8,'head'=4] {'dp'}, dimensions={0}, use_global_device_ids=true | all-gather | bytes 589824 | tf_op jit(solution)/shard_map/all_gather | solution.py:176
  52.9 55.0 %all-gather.1 = bf16[32,1,256]{2,1,0:T(2,128)(2,1)S(1)} all-gather(bf16[1,1,256]{2,1,0:T(2,128)(2,1)S(1)} %reshape.303), channel_id=2, replica_groups=mesh['dp'=8,'head'=4] {'dp','head'}, dimensions={0}, use_global_device_ids=true | all-gather | bytes 16896 | tf_op jit(solution)/shard_map/all_gather | solution.py:174
  120.0 4.9 pad.4
  124.9 5.9 reshape.263
  139.0 17.4 %collective-permute-done.4 = bf16[2,256,1024]{2,1,0:T(8,128)(2,1)S(1)} collective-permute-done((bf16[2,256,1024]{2,1,0:T(8,128)(2,1)S(1)}, bf16[2,256,1024]{2,1,0:T(8,128)(2,1)S(1)}, u32[]{:S(2)}, u32[]{:S(2)}) %collective-permute-start.4) | collective-permute-done | bytes 1048608 | tf_op jit(solution)/shard_map/ppermute | solution.py:38
  181.3 6.1 shard_map.298
  187.4 6.4 shard_map.300
  203.1 5.0 gather_fusion.1
  208.1 4.8 broadcast_select_fusion
  220.1 6.3 shard_map.301
  234.2 6.6 %shard_map.299 = (bf16[512,256]{1,0:T(8,128)(2,1)}, f32[2,1,512]{2,1,0:T(1,128)}) custom-call(f32[2]{0:T(128)} %power_multiply_fusion.slope_ref, bf16[512,256]{1,0:T(8,128)(2,1)} %fusion.16.q_ref, bf16[1536,512]{1,0:T(8,128)(2,1)} %convolution_convert_fusion.2.kv_ref, f32[1024,512]{1,0:T(8,128)} %log-plus-one_select_fusion.near_ref, ...), custom_call_target="tpu_custom_call" | custom-call | flops 805306368 | bytes 6291456 | tf_op jit(solution)/shard_map/pallas_call | solution.py:99
  262.0 4.8 convert_reduce_fusion.2
  298.5 16.0 %collective-permute-done.10 = bf16[512,1024]{1,0:T(8,128)(2,1)S(1)} collective-permute-done((bf16[512,1024]{1,0:T(8,128)(2,1)S(1)}, bf16[512,1024]{1,0:T(8,128)(2,1)S(1)}, u32[]{:S(2)}, u32[]{:S(2)}) %collective-permute-start.10) | collective-permute-done | bytes 1048608 | tf_op jit(solution)/shard_map/ppermute | solution.py:38
  315.9 20.0 %collective-permute-done.8 = bf16[512,1024]{1,0:T(8,128)(2,1)S(1)} collective-permute-done((bf16[512,1024]{1,0:T(8,128)(2,1)S(1)}, bf16[512,1024]{1,0:T(8,128)(2,1)S(1)}, u32[]{:S(2)}, u32[]{:S(2)}) %collective-permute-start.8) | collective-permute-done | bytes 1048608 | tf_op jit(solution)/shard_map/ppermute | solution.py:38
  359.8 8.4 %collective-permute-done.20 = bf16[8,32,1024]{2,1,0:T(8,128)(2,1)S(1)} collective-permute-done((bf16[8,32,1024]{2,1,0:T(8,128)(2,1)S(1)}, bf16[8,32,1024]{2,1,0:T(8,128)(2,1)S(1)}, u32[]{:S(2)}, u32[]{:S(2)}) %collective-permute-start.20) | collective-permute-done | bytes 524320 | tf_op jit(solution)/shard_map/ppermute | solution.py:38
  377.3 5.6 fusion.60
  387.6 7.9 %shard_map.303 = (bf16[512,256]{1,0:T(8,128)(2,1)}, bf16[1536,512]{1,0:T(8,128)(2,1)}) custom-call(f32[2]{0:T(128)} %power_multiply_fusion.slope_ref, bf16[512,256]{1,0:T(8,128)(2,1)} %fusion.16.q_ref, bf16[1536,512]{1,0:T(8,128)(2,1)} %convolution_convert_fusion.2.kv_ref, f32[1024,512]{1,0:T(8,128)} %log-plus-one_select_fusion.near_ref, ...), custom_call_target="tpu_custom_call" | custom-call | flops 2013265920 | bytes 8388608 | tf_op jit(solution)/shard_map/pallas_call | solution.py:111
  395.5 8.0 %shard_map.302 = (bf16[512,256]{1,0:T(8,128)(2,1)}, bf16[1536,512]{1,0:T(8,128)(2,1)}) custom-call(f32[2]{0:T(128)} %power_multiply_fusion.1.slope_ref, bf16[512,256]{1,0:T(8,128)(2,1)} %fusion.17.q_ref, bf16[1536,512]{1,0:T(8,128)(2,1)} %convolution_convert_fusion.3.kv_ref, f32[1024,512]{1,0:T(8,128)} %log-plus-one_select_fusion.near_ref, ...), custom_call_target="tpu_custom_call" | custom-call | flops 2013265920 | bytes 8388608 | tf_op jit(solution)/shard_map/pallas_call | solution.py:111
  427.9 8.2 %shard_map.305 = (bf16[512,256]{1,0:T(8,128)(2,1)}, bf16[1536,512]{1,0:T(8,128)(2,1)}) custom-call(f32[2]{0:T(128)} %power_multiply_fusion.slope_ref, bf16[512,256]{1,0:T(8,128)(2,1)} %fusion.14.q_ref, bf16[1536,512]{1,0:T(8,128)(2,1)} %convolution_convert_fusion.kv_ref, f32[1024,512]{1,0:T(8,128)} %log-plus-one_select_fusion.near_ref, ...), custom_call_target="tpu_custom_call" | custom-call | flops 2013265920 | bytes 8388608 | tf_op jit(solution)/shard_map/pallas_call | solution.py:111
  454.2 5.1 collective-permute-done.24
  459.5 8.0 %shard_map.304 = (bf16[512,256]{1,0:T(8,128)(2,1)}, bf16[1536,512]{1,0:T(8,128)(2,1)}) custom-call(f32[2]{0:T(128)} %power_multiply_fusion.1.slope_ref, bf16[512,256]{1,0:T(8,128)(2,1)} %fusion.15.q_ref, bf16[1536,512]{1,0:T(8,128)(2,1)} %convolution_convert_fusion.1.kv_ref, f32[1024,512]{1,0:T(8,128)} %log-plus-one_select_fusion.near_ref, ...), custom_call_target="tpu_custom_call" | custom-call | flops 2013265920 | bytes 8388608 | tf_op jit(solution)/shard_map/pallas_call | solution.py:111
  485.3 23.0 %collective-permute-done.15 = f32[32,32]{1,0:T(8,128)S(1)} collective-permute-done((f32[32,32]{1,0:T(8,128)S(1)}, f32[32,32]{1,0:T(8,128)S(1)}, u32[]{:S(2)}, u32[]{:S(2)}) %collective-permute-start.15) | collective-permute-done | bytes 4128 | tf_op jit(solution)/shard_map/ppermute | solution.py:38
  527.8 42.9 %reduce-scatter.15.cloned.1.call-done = bf16[128,1024]{1,0:T(8,128)(2,1)} async-done(((bf16[1024,1024]{1,0:T(8,128)(2,1)}), bf16[128,1024]{1,0:T(8,128)(2,1)}) %reduce-scatter.15.cloned.1.call-update) | async-done | bytes 262160
  572.7 65.7 %reduce-scatter.13.cloned.1.call-done = bf16[128,768]{1,0:T(8,128)(2,1)} async-done(((bf16[1024,768]{1,0:T(8,128)(2,1)}), bf16[128,768]{1,0:T(8,128)(2,1)}) %reduce-scatter.13.cloned.1.call-update) | async-done | bytes 196624
  (377 shorter events, 258.4 us)
Async XLA Ops:
  7.2 164.6 %all-gather.7.cloned.1.call-start = ((), (), s32[]{:S(2)}) async-start(), calls=%async_computation.4 | async-start | bytes 1769472 | tf_op jit(solution)/shard_map/all_gather | solution.py:170
  11.8 182.7 %all-gather.13.cloned.1.call-start = ((), (), s32[]{:S(2)}) async-start(), calls=%async_computation.9 | async-start | bytes 1769472 | tf_op jit(solution)/shard_map/all_gather | solution.py:186
  12.6 200.3 %all-gather.9.cloned.1.call-start = ((), (), s32[]{:S(2)}) async-start(), calls=%async_computation.5 | async-start | bytes 2359296 | tf_op jit(solution)/shard_map/all_gather | solution.py:182
  13.3 200.0 %all-gather.11.cloned.1.call-start = ((), (), s32[]{:S(2)}) async-start(), calls=%async_computation.6 | async-start | bytes 2359296 | tf_op jit(solution)/shard_map/all_gather | solution.py:183
  13.4 123.8 %collective-permute-start.1 = (bf16[512,1024]{1,0:T(8,128)(2,1)}, bf16[512,1024]{1,0:T(8,128)(2,1)S(1)}, u32[]{:S(2)}, u32[]{:S(2)}) collective-permute-start(bf16[512,1024]{1,0:T(8,128)(2,1)} %param.21), channel_id=1, source_target_pairs={{0,2},{1,3},{2,0},{3,1},{4,6},{5,7},{6,4},{7,5},{8,10},{9,11},{10,... | collective-permute-start | bytes 3145736 | tf_op jit(solution)/shard_map/ppermute | solution.py:38
  49.3 81.5 %collective-permute-start.3 = (bf16[256,1024]{1,0:T(8,128)(2,1)S(1)}, bf16[256,1024]{1,0:T(8,128)(2,1)S(1)}, u32[]{:S(2)}, u32[]{:S(2)}) collective-permute-start(bf16[256,1024]{1,0:T(8,128)(2,1)S(1)} %all_gather.20), channel_id=1, source_target_pairs={{0,1},{1,0},{2,3},{3,2},{4,5},{5,4},{6,7},{7,6},{8,9},{9,8},{10,11... | collective-permute-start | bytes 1572872 | tf_op jit(solution)/shard_map/ppermute | solution.py:42
  49.3 226.0 %collective-permute-start.9 = (bf16[512,1024]{1,0:T(8,128)(2,1)}, bf16[512,1024]{1,0:T(8,128)(2,1)}, u32[]{:S(2)}, u32[]{:S(2)}) collective-permute-start(bf16[512,1024]{1,0:T(8,128)(2,1)} %param.39), channel_id=1, source_target_pairs={{0,2},{1,3},{2,0},{3,1},{4,6},{5,7},{6,4},{7,5},{8,10},{9,11},{10,... | collective-permute-start | bytes 3145736 | tf_op jit(solution)/shard_map/ppermute | solution.py:38
  49.3 475.2 %reduce-scatter.9.cloned.1.call-start = ((), (), s32[]{:S(2)}) async-start(), calls=%async_computation.7 | async-start | bytes 589824 | tf_op jit(solution)/shard_map/reduce_scatter | solution.py:279
  138.7 61.0 %collective-permute-start.28 = (bf16[2,512,1024]{2,1,0:T(8,128)(2,1)}, bf16[2,512,1024]{2,1,0:T(8,128)(2,1)}, u32[]{:S(2)}, u32[]{:S(2)}) collective-permute-start(bf16[2,512,1024]{2,1,0:T(8,128)(2,1)} %pad_maximum_fusion.4), channel_id=1, source_target_pairs={{0,1},{1,0},{2,3},{3,2},{4,5},{5,4},{6,7},{7,6},{8,9},{9,8},{10,11... | collective-permute-start | bytes 6291464 | tf_op jit(solution)/shard_map/ppermute | solution.py:42
  171.8 41.6 %collective-permute-start = (bf16[1024,768]{1,0:T(8,128)(2,1)}, bf16[1024,768]{1,0:T(8,128)(2,1)}, u32[]{:S(2)}, u32[]{:S(2)}) collective-permute-start(bf16[1024,768]{1,0:T(8,128)(2,1)} %all-gather.7.cloned.1.call-done), channel_id=1, source_target_pairs={{0,1},{1,0},{2,3},{3,2},{4,5},{5,4},{6,7},{7,6},{8,9},{9,8},{10,11... | collective-permute-start | bytes 4718600 | tf_op jit(solution)/shard_map/ppermute | solution.py:42
  212.9 46.3 %collective-permute-start.5 = (bf16[1024,1024]{1,0:T(8,128)(2,1)}, bf16[1024,1024]{1,0:T(8,128)(2,1)}, u32[]{:S(2)}, u32[]{:S(2)}) collective-permute-start(bf16[1024,1024]{1,0:T(8,128)(2,1)} %all-gather.9.cloned.1.call-done), channel_id=1, source_target_pairs={{0,1},{1,0},{2,3},{3,2},{4,5},{5,4},{6,7},{7,6},{8,9},{9,8},{10,11... | collective-permute-start | bytes 6291464 | tf_op jit(solution)/shard_map/ppermute | solution.py:42
  213.3 48.7 %collective-permute-start.6 = (bf16[1024,1024]{0,1:T(8,128)(2,1)}, bf16[1024,1024]{0,1:T(8,128)(2,1)}, u32[]{:S(2)}, u32[]{:S(2)}) collective-permute-start(bf16[1024,1024]{0,1:T(8,128)(2,1)} %all-gather.11.cloned.1.call-done), channel_id=1, source_target_pairs={{0,1},{1,0},{2,3},{3,2},{4,5},{5,4},{6,7},{7,6},{8,9},{9,8},{10,11... | collective-permute-start | bytes 6291464 | tf_op jit(solution)/shard_map/ppermute | solution.py:42
  244.1 26.2 %collective-permute-start.7 = (bf16[512,1024]{1,0:T(8,128)(2,1)S(1)}, bf16[512,1024]{1,0:T(8,128)(2,1)S(1)}, u32[]{:S(2)}, u32[]{:S(2)}) collective-permute-start(bf16[512,1024]{1,0:T(8,128)(2,1)S(1)} %add_convert_fusion.9), channel_id=1, source_target_pairs={{0,2},{1,3},{2,0},{3,1},{4,6},{5,7},{6,4},{7,5},{8,10},{9,11},{10,... | collective-permute-start | bytes 3145736 | tf_op jit(solution)/shard_map/ppermute | solution.py:38
  288.4 26.1 %collective-permute-start.10 = (bf16[512,1024]{1,0:T(8,128)(2,1)S(1)}, bf16[512,1024]{1,0:T(8,128)(2,1)S(1)}, u32[]{:S(2)}, u32[]{:S(2)}) collective-permute-start(bf16[512,1024]{1,0:T(8,128)(2,1)S(1)} %add_convert_fusion.6), channel_id=1, source_target_pairs={{0,2},{1,3},{2,0},{3,1},{4,6},{5,7},{6,4},{7,5},{8,10},{9,11},{10,... | collective-permute-start | bytes 3145736 | tf_op jit(solution)/shard_map/ppermute | solution.py:38
  294.6 41.3 %collective-permute-start.8 = (bf16[512,1024]{1,0:T(8,128)(2,1)S(1)}, bf16[512,1024]{1,0:T(8,128)(2,1)S(1)}, u32[]{:S(2)}, u32[]{:S(2)}) collective-permute-start(bf16[512,1024]{1,0:T(8,128)(2,1)S(1)} %add_convert_fusion.8), channel_id=1, source_target_pairs={{0,2},{1,3},{2,0},{3,1},{4,6},{5,7},{6,4},{7,5},{8,10},{9,11},{10,... | collective-permute-start | bytes 3145736 | tf_op jit(solution)/shard_map/ppermute | solution.py:38
  359.6 57.1 %collective-permute-start.27 = (bf16[1024,1024]{0,1:T(8,128)(2,1)}, bf16[1024,1024]{0,1:T(8,128)(2,1)}, u32[]{:S(2)}, u32[]{:S(2)}) collective-permute-start(bf16[1024,1024]{0,1:T(8,128)(2,1)} %fusion.3), channel_id=1, source_target_pairs={{0,1},{1,0},{2,3},{3,2},{4,5},{5,4},{6,7},{7,6},{8,9},{9,8},{10,11... | collective-permute-start | bytes 6291464 | tf_op jit(solution)/shard_map/ppermute | solution.py:42
  369.2 156.8 %reduce-scatter.11.cloned.1.call-start = ((), (), s32[]{:S(2)}) async-start(), calls=%async_computation.8 | async-start | bytes 2359296 | tf_op jit(solution)/shard_map/reduce_scatter | solution.py:259
  376.5 194.2 %reduce-scatter.15.cloned.1.call-start = ((), (), s32[]{:S(2)}) async-start(), calls=%async_computation.11 | async-start | bytes 2359296
  385.0 41.0 %collective-permute-start.11 = (bf16[512,512]{1,0:T(8,128)(2,1)}, bf16[512,512]{1,0:T(8,128)(2,1)}, u32[]{:S(2)}, u32[]{:S(2)}) collective-permute-start(bf16[512,512]{1,0:T(8,128)(2,1)} %slice.183), channel_id=1, source_target_pairs={{0,2},{1,3},{2,0},{3,1},{4,6},{5,7},{6,4},{7,5},{8,10},{9,11},{10,... | collective-permute-start | bytes 1572872 | tf_op jit(solution)/shard_map/ppermute | solution.py:38
  386.7 59.2 %collective-permute-start.21 = (f32[32,224]{1,0:T(8,128)S(1)}, f32[32,224]{1,0:T(8,128)S(1)}, u32[]{:S(2)}, u32[]{:S(2)}) collective-permute-start(f32[32,224]{1,0:T(8,128)S(1)} %pad_maximum_fusion.12), channel_id=1, source_target_pairs={{0,1},{1,0},{2,3},{3,2},{4,5},{5,4},{6,7},{7,6},{8,9},{9,8},{10,11... | collective-permute-start | bytes 86024 | tf_op jit(solution)/shard_map/ppermute | solution.py:42
  425.9 212.4 %reduce-scatter.13.cloned.1.call-start = ((), (), s32[]{:S(2)}) async-start(), calls=%async_computation.10 | async-start | bytes 1769472
  442.7 26.2 %collective-permute-start.13 = (bf16[1024,768]{0,1:T(8,128)(2,1)}, bf16[1024,768]{0,1:T(8,128)(2,1)}, u32[]{:S(2)}, u32[]{:S(2)}) collective-permute-start(bf16[1024,768]{0,1:T(8,128)(2,1)} %pad_maximum_fusion.5), channel_id=1, source_target_pairs={{0,1},{1,0},{2,3},{3,2},{4,5},{5,4},{6,7},{7,6},{8,9},{9,8},{10,11... | collective-permute-start | bytes 4718600 | tf_op jit(solution)/shard_map/ppermute | solution.py:42
  459.3 49.3 %collective-permute-start.25 = (f32[32,224]{1,0:T(8,128)S(1)}, f32[32,224]{1,0:T(8,128)S(1)}, u32[]{:S(2)}, u32[]{:S(2)}) collective-permute-start(f32[32,224]{1,0:T(8,128)S(1)} %add.614), channel_id=1, source_target_pairs={{0,16},{4,20},{8,24},{12,28},{16,0},{20,4},{24,8},{28,12},{1,17},{... | collective-permute-start | bytes 86024 | tf_op jit(solution)/shard_map/ppermute | solution.py:135
  482.6 39.2 %collective-permute-start.12 = (bf16[512,1024]{1,0:T(8,128)(2,1)S(1)}, bf16[512,1024]{1,0:T(8,128)(2,1)S(1)}, u32[]{:S(2)}, u32[]{:S(2)}) collective-permute-start(bf16[512,1024]{1,0:T(8,128)(2,1)S(1)} %add_convert_fusion.5), channel_id=1, source_target_pairs={{0,2},{1,3},{2,0},{3,1},{4,6},{5,7},{6,4},{7,5},{8,10},{9,11},{10,... | collective-permute-start | bytes 3145736 | tf_op jit(solution)/shard_map/ppermute | solution.py:38
  (79 other events, 613.6 us)
Sparse Core Ops, SparseCore 0:
  12.0 48.4 all-gather.6
  62.6 43.1 all-gather.12
  108.0 48.0 all-gather.8
  158.0 49.5 all-gather.10
  369.4 59.0 reduce-scatter.8
  432.2 67.2 reduce-scatter.10
  503.5 67.1 reduce-scatter.14
  574.5 63.7 reduce-scatter.12

commit v2 on v1

v2 whole, which is shorter than its diff:
```python
import jax
import jax.numpy as jnp
from jax import lax
from jax.experimental import pallas as pl
from jax.experimental.pallas import tpu as pltpu
from jax.sharding import PartitionSpec as P

D = 1024
HD = 128
SEG = 512
CM = 512
RATE = 3
CC = 171
LN_EPS = 1e-05
LOG2E = 1.4426950408889634
SCALE2 = LOG2E * HD ** (-0.5)
FAR = 1e32
VMEM = 56 * 1024 * 1024
BF = jnp.bfloat16
F32 = jnp.float32


def nt(a, b):
    return lax.dot_general(a, b, (((1,), (1,)), ((), ())), preferred_element_type=F32)


def tn(a, b):
    return lax.dot_general(a, b, (((0,), (0,)), ((), ())), preferred_element_type=F32)


def nn(a, b):
    return jnp.dot(a, b, preferred_element_type=F32)


def x_swap(a):
    return lax.ppermute(a, "head", [(i, i ^ 2) for i in range(4)])


def c_swap(a):
    return lax.ppermute(a, "head", [(i, i ^ 1) for i in range(4)])


def fwd_kernel(slope_ref, q_ref, kv_ref, near_ref, far_ref, mixed_ref, lse_ref):
    a = pl.program_id(0)
    slope2 = slope_ref[a] * LOG2E
    q = q_ref[0]
    parts = []
    for n in range(3):
        k = kv_ref[0, n * SEG:(n + 1) * SEG, :HD]
        table = far_ref[...] if n == 0 else near_ref[(n - 1) * SEG:n * SEG, :]
        parts.append(nt(k, q) * SCALE2 - slope2 * table)
    top = jnp.maximum(jnp.maximum(jnp.max(parts[0], axis=0, keepdims=True), jnp.max(parts[1], axis=0, keepdims=True)),
                      jnp.max(parts[2], axis=0, keepdims=True))
    total = jnp.zeros((1, SEG), F32)
    acc = jnp.zeros((HD, SEG), F32)
    for n in range(3):
        p = jnp.exp2(parts[n] - top)
        total = total + jnp.sum(p, axis=0, keepdims=True)
        acc = acc + tn(kv_ref[0, n * SEG:(n + 1) * SEG, HD:], p.astype(BF))
    mixed_ref[...] = (acc / total).T.astype(BF)
    lse_ref[...] = (top + jnp.log2(total)).reshape(1, 1, SEG)


def bwd_kernel(slope_ref, q_ref, kv_ref, near_ref, far_ref, mixed_ref, lse_ref, do_ref, dq_ref, dkv_ref, sum_ref):
    a = pl.program_id(0)
    slope2 = slope_ref[a] * LOG2E
    q = q_ref[0]
    do = do_ref[...]
    lse = lse_ref[...].reshape(1, SEG)
    row_dot = jnp.sum((do.astype(F32) * mixed_ref[...].astype(F32)).T, axis=0, keepdims=True)
    inv_root = HD ** (-0.5)
    dq = jnp.zeros((HD, SEG), F32)
    for n in range(3):
        rows = slice(n * SEG, (n + 1) * SEG)
        k = kv_ref[0, rows, :HD]
        v = kv_ref[0, rows, HD:]
        table = far_ref[...] if n == 0 else near_ref[(n - 1) * SEG:n * SEG, :]
        p = jnp.exp2(nt(k, q) * SCALE2 - slope2 * table - lse)
        ds = (p * (nt(v, do) - row_dot)).astype(BF)
        dkv_ref[rows, HD:] = nn(p.astype(BF), do).astype(BF)
        dkv_ref[rows, :HD] = (nn(ds, q) * inv_root).astype(BF)
        dq = dq + tn(k, ds)
    dq = (dq.T * inv_root).astype(BF)
    dq_ref[...] = dq
    sum_ref[...] = jnp.sum(dq.astype(F32), axis=0, keepdims=True)


def ring_order(n):
    up = list(range(0, n, 2))
    return up + [p + 1 for p in reversed(up)]


def ring_perms(n):
    order = ring_order(n)
    ahead = [(order[p], order[(p + 1) % n]) for p in range(n)]
    return ahead, [(b, a) for a, b in ahead]


def ring_place(d, n):
    return jnp.where(d % 2 == 0, d // 2, n - 1 - d // 2)


def ring_member(p, n):
    p = p % n
    return jnp.where(p < n // 2, 2 * p, 2 * (n - 1 - p) + 1)


def ring_gather(chunk, n):
    ahead, back = ring_perms(n)
    out, f, b = [chunk], chunk, chunk
    for k in range(1, n // 2 + 1):
        f = lax.ppermute(f, "dp", ahead)
        out.append(f)
        if k < n - n // 2:
            b = lax.ppermute(b, "dp", back)
            out.append(b)
    return out


def ring_sources(d, n):
    place = ring_place(d, n)
    steps = [0]
    for k in range(1, n // 2 + 1):
        steps.append(-k)
        if k < n - n // 2:
            steps.append(k)
    return ring_member(place + jnp.array(steps, jnp.int32), n).astype(jnp.int32)


def ring_scatter(array, d, n):
    ahead, back = ring_perms(n)
    place = ring_place(d, n)

    def block(p):
        return lax.dynamic_index_in_dim(array, ring_member(p, n), 0, keepdims=False).astype(F32)

    up, down = n // 2, n - n // 2 - 1
    f, b = block(place + up).astype(BF), block(place - down).astype(BF)
    for k in range(1, up + 1):
        f = lax.ppermute(f, "dp", ahead)
        if k < up:
            f = (f.astype(F32) + block(place + up - k)).astype(BF)
        if k <= down:
            b = lax.ppermute(b, "dp", back)
            if k < down:
                b = (b.astype(F32) + block(place - down + k)).astype(BF)
    return f.astype(F32) + b.astype(F32) + block(place)


ROWS = 3 * SEG
HALF = D // 2
smem_spec = pl.BlockSpec(memory_space=pltpu.SMEM)
vmem_spec = pl.BlockSpec(memory_space=pltpu.VMEM)
any_spec = pl.BlockSpec(memory_space=pl.ANY)


def params():
    return pltpu.CompilerParams(vmem_limit_bytes=VMEM)


def cost(us):
    return pl.CostEstimate(flops=int(us * 1.1e9), bytes_accessed=1 << 20, transcendentals=0)


def shape(*dims, kind=BF):
    return jax.ShapeDtypeStruct(dims, kind)


def whole(*dims):
    return pl.BlockSpec(dims, lambda *i: (0,) * len(dims))


def attend(t, slopes, q, kv, near, far):
    return pl.pallas_call(
        fwd_kernel,
        grid=(4,),
        in_specs=[
            smem_spec,
            pl.BlockSpec((1, SEG, HD), lambda a: (t, 0, a)),
            pl.BlockSpec((1, ROWS, 2 * HD), lambda a: (t, 0, a)),
            whole(2 * SEG, SEG),
            whole(SEG, SEG),
        ],
        out_specs=[pl.BlockSpec((SEG, HD), lambda a: (0, a)), pl.BlockSpec((1, 1, SEG), lambda a: (a, 0, 0))],
        out_shape=[shape(SEG, HALF), shape(4, 1, SEG, kind=F32)],
        compiler_params=params(),
        cost_estimate=cost(12),
    )(slopes, q, kv, near, far)


def attend_back(t, slopes, q, kv, near, far, mixed, lse, do):
    column = pl.BlockSpec((SEG, HD), lambda a: (0, a))
    return pl.pallas_call(
        bwd_kernel,
        grid=(4,),
        in_specs=[
            smem_spec,
            pl.BlockSpec((1, SEG, HD), lambda a: (t, 0, a)),
            pl.BlockSpec((1, ROWS, 2 * HD), lambda a: (t, 0, a)),
            whole(2 * SEG, SEG),
            whole(SEG, SEG),
            column,
            pl.BlockSpec((1, 1, SEG), lambda a: (a, 0, 0)),
            column,
        ],
        out_specs=[column, pl.BlockSpec((ROWS, 2 * HD), lambda a: (0, a)), pl.BlockSpec((1, HD), lambda a: (0, a))],
        out_shape=[shape(SEG, HALF), shape(ROWS, D), shape(1, HALF, kind=F32)],
        compiler_params=params(),
        cost_estimate=cost(16),
    )(slopes, q, kv, near, far, mixed, lse, do)


def project_kernel(ids_ref, comp_ref, mem_ref, own_ref, other_ref, w_own_ref, w_par_ref, bias_ref, kv_ref, q_ref):
    t, n = pl.program_id(0), pl.program_id(1)

    def put(source):
        kv_ref[0, :, :HALF] = nn(source, w_own_ref[:, :HALF]).astype(BF)
        kv_ref[0, :, HALF:] = nn(source, w_par_ref[:, :HALF]).astype(BF)

    def ask(source):
        put(source)
        q_ref[0, :, :2 * HD] = (nn(source, w_own_ref[:, HALF:]) + bias_ref[:, :2 * HD]).astype(BF)
        q_ref[0, :, 2 * HD:] = (nn(source, w_par_ref[:, HALF:]) + bias_ref[:, 2 * HD:]).astype(BF)

    pl.when(n == 0)(lambda: put(comp_ref[0]))
    pl.when(n == 1)(lambda: put(mem_ref[0]))
    pl.when((n == 2) & (t == 0))(lambda: ask(own_ref[...]))
    pl.when((n == 2) & (t == 1))(lambda: ask(other_ref[...]))


def project(ids, compressed, memory, own, other, w_own, w_par, bias):
    return pl.pallas_call(
        project_kernel,
        grid_spec=pltpu.PrefetchScalarGridSpec(
            num_scalar_prefetch=1,
            grid=(2, 3),
            in_specs=[
                pl.BlockSpec((1, CM, D), lambda t, n, ids: (ids[t], 0, 0)),
                pl.BlockSpec((1, SEG, D), lambda t, n, ids: (ids[t], 0, 0)),
                whole(SEG, D),
                whole(SEG, D),
                whole(D, 3 * 2 * HD),
                whole(D, 3 * 2 * HD),
                whole(1, HALF),
            ],
            out_specs=[
                pl.BlockSpec((1, SEG, D), lambda t, n, ids: (t, n, 0)),
                pl.BlockSpec((1, SEG, HALF), lambda t, n, ids: (t, 0, 0)),
            ],
        ),
        out_shape=[shape(2, ROWS, D), shape(2, SEG, HALF)],
        compiler_params=params(),
        cost_estimate=cost(12),
    )(ids, compressed, memory, own, other, w_own, w_par, bias)


def norm_kernel(mixed_ref, sent_ref, w_ref, in_ref, gain_ref, shift_ref, residual_ref, normed_ref):
    out = nn(mixed_ref[...], w_ref[:HALF]) + nn(sent_ref[...], w_ref[HALF:])
    residual = in_ref[...].astype(F32) + out
    residual_ref[...] = residual
    center = residual - jnp.mean(residual, axis=-1, keepdims=True)
    rstd = lax.rsqrt(jnp.mean(center * center, axis=-1, keepdims=True) + LN_EPS)
    normed_ref[...] = (center * rstd * gain_ref[...] + shift_ref[...]).astype(BF)


def attention_out(mixed, sent, w_o, inputs, gain, shift):
    rows = SEG // 2
    half = pl.BlockSpec((rows, HALF), lambda i: (i, 0))
    full = pl.BlockSpec((rows, D), lambda i: (i, 0))
    return pl.pallas_call(
        norm_kernel,
        grid=(2,),
        in_specs=[half, half, whole(D, D), full, whole(1, D), whole(1, D)],
        out_specs=[full, full],
        out_shape=[shape(SEG, D, kind=F32), shape(SEG, D)],
        compiler_params=params(),
        cost_estimate=cost(4),
    )(mixed, sent, w_o, inputs, gain, shift)


def gelu_pair(before):
    c0, c1 = 0.7978845608028654, 0.044715
    sq = before * before
    t = jnp.tanh(c0 * before * (1.0 + c1 * sq))
    half = 0.5 * (1.0 + t)
    return before * half, half + 0.5 * before * (1.0 - t * t) * (c0 * (1.0 + 3.0 * c1 * sq))


def ffn_kernel(norm_ref, cot_ref, bias_ref, up0, down0, up1, down1, hid_ref, gb_ref, sum_ref, branch_ref, gn_ref, branch, gn):
    i, n = pl.program_id(0), pl.num_programs(0)

    def body(up, down, first):
        before = nn(norm_ref[...], up[...]) + bias_ref[...]
        act, slope = gelu_pair(before)
        act = act.astype(BF)
        gb = (nn(cot_ref[...], down[...]) * slope).astype(BF)
        hid_ref[...] = act
        gb_ref[...] = gb
        sum_ref[...] = jnp.sum(gb.astype(F32), axis=0, keepdims=True)
        if first:
            branch[...] = nt(act, down[...])
            gn[...] = nt(gb, up[...])
        else:
            branch[...] += nt(act, down[...])
            gn[...] += nt(gb, up[...])

    pl.when(i == 0)(lambda: body(up0, down0, True))
    pl.when((i > 0) & (i < n // 2))(lambda: body(up0, down0, False))
    pl.when(i >= n // 2)(lambda: body(up1, down1, False))

    @pl.when(i == n - 1)
    def _():
        branch_ref[...] = branch[...].astype(branch_ref.dtype)
        gn_ref[...] = gn[...].astype(gn_ref.dtype)


def feed_forward(norm, cot, bias, w_own, w_par, kind, tile=512):
    n = D // tile
    low = lambda i: jnp.minimum(i, n - 1)
    high = lambda i: jnp.maximum(i - n, 0)
    part = pl.BlockSpec((SEG, tile), lambda i: (0, i))
    return pl.pallas_call(
        ffn_kernel,
        grid=(2 * n,),
        in_specs=[
            whole(SEG, D),
            whole(SEG, D),
            pl.BlockSpec((1, tile), lambda i: (0, i)),
            pl.BlockSpec((D, tile), lambda i: (0, low(i))),
            pl.BlockSpec((D, tile), lambda i: (1, low(i))),
            pl.BlockSpec((D, tile), lambda i: (0, high(i))),
            pl.BlockSpec((D, tile), lambda i: (1, high(i))),
        ],
        out_specs=[part, part, pl.BlockSpec((1, tile), lambda i: (0, i)), whole(SEG, D), whole(SEG, D)],
        out_shape=[shape(SEG, 2 * D), shape(SEG, 2 * D), shape(1, 2 * D, kind=F32), shape(SEG, D, kind=kind), shape(SEG, D, kind=kind)],
        scratch_shapes=[pltpu.VMEM((SEG, D), F32)] * 2,
        compiler_params=params(),
        cost_estimate=cost(16),
    )(norm, cot, bias, w_own, w_own, w_par, w_par)


def ffn_grad_kernel(n0, n1, c0, c1, gb0, gb1, hid0, hid1, *rest):
    out_ref = rest[-1]

    def put(total):
        total = total.reshape(out_ref.shape[0], out_ref.shape[2], -1)
        if len(rest) > 1:
            total = total + rest[0][:, 0].astype(F32)
        out_ref[:, 0] = total.astype(BF)

    m = pl.program_id(0)
    pl.when(m == 0)(lambda: put(tn(n0[...], gb0[...]) + tn(n1[...], gb1[...])))
    pl.when(m == 1)(lambda: put(tn(c0[...], hid0[...]) + tn(c1[...], hid1[...])))


def ffn_grads(g, n_dp, norms, cots, gbs, hids, *received, tile=512):
    n = D // tile
    tokens = whole(SEG, D)
    early = pl.BlockSpec((SEG, tile), lambda m, i: (0, g * n + jnp.where(m == 0, i, n - 1)))
    late = pl.BlockSpec((SEG, tile), lambda m, i: (0, g * n + jnp.where(m == 0, 0, i)))
    block = pl.BlockSpec((n_dp, 1, D // n_dp, tile), lambda m, i: (0, m, 0, i))
    return pl.pallas_call(
        ffn_grad_kernel,
        grid=(2, n),
        in_specs=[tokens] * 4 + [early] * 2 + [late] * 2 + [block] * len(received),
        out_specs=block,
        out_shape=shape(n_dp, 2, D // n_dp, D),
        compiler_params=params(),
        cost_estimate=cost(7),
    )(*norms, *cots, *gbs, *hids, *received)


def norm_back_kernel(h_ref, residual_ref, gn_ref, gnx_ref, cot_ref, gain_ref, mixed_ref, sent_ref, w_ref,
                     grad_ref, keep_ref, send_ref, sums_ref, out_ref, acc):
    i = pl.program_id(0)
    residual = residual_ref[...]
    center = residual - jnp.mean(residual, axis=-1, keepdims=True)
    rstd = lax.rsqrt(jnp.mean(center * center, axis=-1, keepdims=True) + LN_EPS)
    xhat = center * rstd
    gn = gn_ref[...] + gnx_ref[...].astype(F32)
    g = gn * gain_ref[...]
    cot = cot_ref[...].astype(F32)
    grad = cot + rstd * (g - jnp.mean(g, axis=-1, keepdims=True) - xhat * jnp.mean(g * xhat, axis=-1, keepdims=True))
    grad_ref[...] = grad
    low = grad.astype(BF)
    keep_ref[...] = nt(low, w_ref[:HALF]).astype(BF)
    send_ref[...] = nt(low, w_ref[HALF:]).astype(BF)
    total = lambda a: jnp.sum(a, axis=0, keepdims=True)
    sums = jnp.concatenate([total(gn * xhat), total(gn), total(cot)], axis=0)

    @pl.when(i == 0)
    def _():
        sums_ref[...] = sums
        acc[:HALF] = tn(mixed_ref[...], low)
        acc[HALF:] = tn(sent_ref[...], low)

    @pl.when(i > 0)
    def _():
        sums_ref[...] += sums
        acc[:HALF] += tn(mixed_ref[...], low)
        acc[HALF:] += tn(sent_ref[...], low)

    @pl.when(i == pl.num_programs(0) - 1)
    def _():
        for b in range(4):
            out_ref[h_ref[0] ^ b] = acc[b * 2 * HD:(b + 1) * 2 * HD].astype(BF)


def norm_back(h, residual, gn, gnx, cot, gain, mixed, sent, w_o):
    rows = SEG // 2
    half = pl.BlockSpec((rows, HALF), lambda i: (i, 0))
    full = pl.BlockSpec((rows, D), lambda i: (i, 0))
    return pl.pallas_call(
        norm_back_kernel,
        grid=(2,),
        in_specs=[smem_spec, full, full, full, full, whole(1, D), half, half, whole(D, D)],
        out_specs=[full, half, half, whole(3, D), whole(4, 2 * HD, D)],
        out_shape=[shape(SEG, D, kind=F32), shape(SEG, HALF), shape(SEG, HALF), shape(3, D, kind=F32), shape(4, 2 * HD, D)],
        scratch_shapes=[pltpu.VMEM((D, D), F32)],
        compiler_params=params(),
        cost_estimate=cost(7),
    )(h, residual, gn, gnx, cot, gain, mixed, sent, w_o)


def term_kernel(dq_ref, dkv_ref, w_own_ref, w_par_ref, *rest):
    out = nt(dkv_ref[:, :HALF], w_own_ref[:, :HALF]) + nt(dkv_ref[:, HALF:], w_par_ref[:, :HALF])
    out = out + nt(dq_ref[:, :2 * HD], w_own_ref[:, HALF:]) + nt(dq_ref[:, 2 * HD:], w_par_ref[:, HALF:])
    if len(rest) > 1:
        out = out + rest[0][...]
    rest[-1][...] = out.astype(rest[-1].dtype)


def token_term(dq, dkv, w_own, w_par, *residual):
    rows = SEG // 2
    full = pl.BlockSpec((rows, D), lambda i: (i, 0))
    weight = whole(D, 3 * 2 * HD)
    return pl.pallas_call(
        term_kernel,
        grid=(2,),
        in_specs=[
            pl.BlockSpec((rows, HALF), lambda i: (i, 0)),
            pl.BlockSpec((rows, D), lambda i: (4 + i, 0)),
            weight,
            weight,
        ] + [full] * len(residual),
        out_specs=full,
        out_shape=shape(SEG, D, kind=F32 if residual else BF),
        compiler_params=params(),
        cost_estimate=cost(4),
    )(dq, dkv, w_own, w_par, *residual)


def weight_grad_kernel(ids_ref, comp_ref, mem_ref, own_ref, other_ref, dkv0, dkv1, dq0, dq1, *rest):
    t, n = pl.program_id(0), pl.program_id(1)
    out_ref, acc = rest[-2:]
    rows = D // out_ref.shape[0]

    def add(source, dkv):
        acc[:, :HALF] += tn(source, dkv[...])

    @pl.when((t == 0) & (n == 0))
    def _():
        acc[:, :HALF] = tn(comp_ref[0], dkv0[...])

    pl.when((t == 0) & (n == 1))(lambda: add(mem_ref[0], dkv0))

    @pl.when((t == 0) & (n == 2))
    def _():
        add(own_ref[...], dkv0)
        acc[:, HALF:] = tn(own_ref[...], dq0[...])

    pl.when((t == 1) & (n == 0))(lambda: add(comp_ref[0], dkv1))
    pl.when((t == 1) & (n == 1))(lambda: add(mem_ref[0], dkv1))

    @pl.when((t == 1) & (n == 2))
    def _():
        add(other_ref[...], dkv1)
        acc[:, HALF:] += tn(other_ref[...], dq1[...])
        total = acc[...].reshape(out_ref.shape[0], rows, 6 * HD)
        if len(rest) > 2:
            total = total + rest[0][...].astype(F32)
            out_ref[:, rows:] = rest[1][...]
        out_ref[:, :rows] = total.astype(BF)


def weight_grads(g, n_dp, ids, compressed, memory, own, other, dkvs, dqs, *received):
    rows = D // n_dp
    outer = rows + (16 if received else 0)
    return pl.pallas_call(
        weight_grad_kernel,
        grid_spec=pltpu.PrefetchScalarGridSpec(
            num_scalar_prefetch=1,
            grid=(2, 3),
            in_specs=[
                pl.BlockSpec((1, CM, D), lambda t, n, ids: (ids[t], 0, 0)),
                pl.BlockSpec((1, SEG, D), lambda t, n, ids: (ids[t], 0, 0)),
                whole(SEG, D),
                whole(SEG, D),
                pl.BlockSpec((SEG, HALF), lambda t, n, ids: (jnp.where(t == 0, n, 2), g)),
                pl.BlockSpec((SEG, HALF), lambda t, n, ids: (jnp.where(t == 0, 0, n), g)),
                pl.BlockSpec((SEG, 2 * HD), lambda t, n, ids: (0, g)),
                pl.BlockSpec((SEG, 2 * HD), lambda t, n, ids: (0, g)),
            ] + [whole(*a.shape) for a in received],
            out_specs=whole(n_dp, outer, 6 * HD),
            scratch_shapes=[pltpu.VMEM((D, 6 * HD), F32)],
        ),
        out_shape=shape(n_dp, outer, 6 * HD),
        compiler_params=params(),
        cost_estimate=cost(7),
    )(ids, compressed, memory, own, other, *dkvs, *dqs, *received)


def copies(moves, out_shapes, index, *arrays):
    count = len(arrays)

    def kernel(index_ref, *refs):
        ins, outs, sems = refs[:count], refs[count:-1], refs[-1]
        started = []
        for n, (source, target) in enumerate(moves(index_ref, ins, outs)):
            copy = pltpu.make_async_copy(source, target, sems.at[n])
            copy.start()
            started.append(copy)
        for copy in started:
            copy.wait()

    return pl.pallas_call(
        kernel,
        in_specs=[smem_spec] + [any_spec] * count,
        out_specs=[vmem_spec] * len(out_shapes),
        out_shape=[shape(*dims) for dims in out_shapes],
        scratch_shapes=[pltpu.SemaphoreType.DMA((64,))],
        compiler_params=pltpu.CompilerParams(vmem_limit_bytes=16 << 20),
        cost_estimate=cost(3),
    )(index, *arrays)


def assemble(chunks, sources, parts):
    n, cols = len(chunks), chunks[0].shape[1]

    def moves(index, ins, outs):
        for k in range(n):
            row = 0
            for out, rows in zip(outs, parts):
                yield ins[k].at[pl.ds(row, rows)], out.at[pl.ds(pl.multiple_of(index[k] * rows, rows), rows)]
                row += rows

    return copies(moves, [(n * rows, cols) for rows in parts], sources, *chunks)


def compress_kernel(h_ref, memory_ref, compressed_ref, w_ref, bias_ref, out_ref, weight):
    n_dp, _, rows, width = w_ref.shape

    @pl.when(pl.program_id(0) == 0)
    def _():
        for r in range(RATE):
            for k in range(n_dp):
                weight[r, k * rows:(k + 1) * rows] = w_ref[k, r]

    row = lax.broadcasted_iota(jnp.int32, (176, SEG), 0)
    col = lax.broadcasted_iota(jnp.int32, (176, SEG), 1)
    total = jnp.zeros((176, width), F32)
    for r in range(RATE):
        pick = jnp.where((col == RATE * row + r) & (row < CC), 1.0, 0.0).astype(BF)
        taken = nn(pick, memory_ref[0]).astype(BF)
        total = total + nn(taken, weight[r])
    made = (total + bias_ref[...].astype(F32)).astype(BF)
    to = lax.broadcasted_iota(jnp.int32, (SEG, SEG), 0)
    of = lax.broadcasted_iota(jnp.int32, (SEG, SEG), 1)
    keep = jnp.where(of == to + CC, 1.0, 0.0).astype(BF)
    to = lax.broadcasted_iota(jnp.int32, (SEG, 176), 0)
    of = lax.broadcasted_iota(jnp.int32, (SEG, 176), 1)
    put = jnp.where((of == to - (CM - CC)) & (of < CC), 1.0, 0.0).astype(BF)
    out_ref[0] = (nn(keep, compressed_ref[0]) + nn(put, made)).astype(BF)


def compress(h, memory, compressed, w, bias):
    seqs, width = memory.shape[0], w.shape[3]
    return pl.pallas_call(
        compress_kernel,
        grid_spec=pltpu.PrefetchScalarGridSpec(
            num_scalar_prefetch=1,
            grid=(seqs,),
            in_specs=[
                pl.BlockSpec((1, SEG, D), lambda s, h: (s, 0, 0)),
                pl.BlockSpec((1, CM, width), lambda s, h: (s, 0, h[0])),
                whole(*w.shape),
                whole(1, width),
            ],
            out_specs=pl.BlockSpec((1, CM, width), lambda s, h: (s, 0, 0)),
            scratch_shapes=[pltpu.VMEM((RATE, D, width), BF)],
        ),
        out_shape=shape(seqs, CM, width),
        compiler_params=params(),
        cost_estimate=cost(8),
    )(h, memory, compressed, w, bias.reshape(1, -1))


def per_device(
    inputs,
    memory,
    compressed,
    slot_valid,
    slot_age,
    w_query,
    w_key,
    w_value,
    content_bias,
    w_out,
    ln_gain,
    ln_bias,
    w_up,
    up_bias,
    w_down,
    down_bias,
    w_comp,
    comp_bias,
    cotangent,
):
    n_dp = lax.axis_size("dp")
    d = lax.axis_index("dp")
    h = lax.axis_index("head")
    h1 = h.reshape(1)
    ids = jnp.stack([h, h ^ 2]).astype(jnp.int32)
    seqs = memory.shape[0]
    rows = w_key.shape[0]
    out_rows = w_out.shape[0]
    share, up_share = content_bias.shape[0], up_bias.shape[0]
    values = 4 * share + up_share
    sources = ring_sources(d, n_dp)
    pick = lambda a, n, axis: lax.dynamic_index_in_dim(a, n, axis, keepdims=False)

    pack = jnp.concatenate(
        [w_key[:, :HD], w_value[:, :HD], w_key[:, HD:], w_value[:, HD:], w_query], axis=1
    )
    small = jnp.concatenate([content_bias, ln_gain, ln_bias, down_bias, up_bias]).reshape(1, -1)
    small = jnp.concatenate([small, c_swap(small)])
    small = jnp.concatenate([small, x_swap(small)])
    small = jnp.take(small, h ^ jnp.arange(4), axis=0, mode="clip")
    small = jnp.pad(small, ((0, 12), (0, 6 * HD - values)))
    pack_ring = ring_gather(jnp.concatenate([pack, small]), n_dp)
    inputs_x = x_swap(inputs)
    last = jnp.concatenate(
        [w_comp.reshape(RATE * rows, 2 * HD)] + [w_out[:, k * 2 * HD:(k + 1) * 2 * HD] for k in range(4)]
    )
    last = lax.all_gather(last, "dp", axis=0, tiled=True).reshape(n_dp, -1, 2 * HD)
    cot_x = x_swap(cotangent)
    ffn_ring = ring_gather(jnp.concatenate([w_up, w_down.T]), n_dp)

    w_own, small = assemble(pack_ring, sources, (rows, 16))
    w_par = c_swap(w_own)
    small = small.reshape(n_dp, 16, 6 * HD)[:, :4, :values].reshape(4 * n_dp, values).astype(F32)
    bias_all = small[:, :share].reshape(4, 2 * HD)
    gain = small[:, share:2 * share].reshape(1, D)
    shift = small[:, 2 * share:3 * share].reshape(1, D)
    down_shift = small[:, 3 * share:4 * share].reshape(1, D)
    up_shift = small[:, 4 * share:].reshape(4, D)
    two = lambda a: jnp.concatenate([pick(a, h, 0), pick(a, h ^ 1, 0)]).reshape(1, -1)
    bias, up_shift = two(bias_all), two(up_shift)

    i = jnp.arange(SEG, dtype=jnp.int32)[None, :]
    j = jnp.arange(2 * SEG, dtype=jnp.int32)[:, None]
    gap = i + SEG - j
    near = jnp.where(gap >= 0, jnp.log1p(jnp.maximum(gap, 0).astype(F32)), FAR)

    def far_of(s):
        age, valid = pick(slot_age, s, 0)[:, None], pick(slot_valid, s, 0)[:, None]
        return jnp.where(valid > 0, jnp.log1p(jnp.maximum(i + age, 0).astype(F32)), FAR)

    far = [far_of(h), far_of(h ^ 2)]
    heads = jnp.concatenate([2 * h + jnp.arange(2), 2 * (h ^ 1) + jnp.arange(2)])
    slopes = 0.6 * jnp.power(0.7, heads.astype(F32))

    kv_q = project(ids, compressed, memory, inputs, inputs_x, w_own, w_par, bias)
    kv, q = kv_q
    mixed_x, lse_x = attend(1, slopes, q, kv, near, far[1])
    sent = x_swap(mixed_x)
    mixed, lse = attend(0, slopes, q, kv, near, far[0])

    def ffn_moves(index, ins, outs):
        for k in range(n_dp):
            at = pl.multiple_of(index[k] * rows, rows)
            yield ins[k].at[pl.ds(0, rows)], outs[0].at[pl.ds(at, rows)]
            yield ins[k].at[pl.ds(rows, rows)], outs[0].at[pl.ds(D + at, rows)]

    (ffn_own,) = copies(ffn_moves, [(2 * D, D)], sources, *ffn_ring)
    ffn_par = c_swap(ffn_own)

    comp_w = last[:, :RATE * rows].reshape(n_dp, RATE, rows, 2 * HD)
    wo = last[:, RATE * rows:].reshape(n_dp, 4, out_rows, 2 * HD).transpose(0, 2, 1, 3).reshape(n_dp, out_rows, D)
    wo2 = jnp.stack([wo, c_swap(wo)])
    wo2x = x_swap(wo2)
    per = n_dp // 4

    def wo_moves(index, ins, outs):
        me = index[0]
        for e in range(4):
            for b in range(4):
                source = ins[e // 2].at[e % 2, pl.ds(b * per, per)]
                yield source, outs[0].at[me ^ b, :, me ^ e]

    (w_o,) = copies(wo_moves, [(4, per, 4, out_rows, D)], h1, wo2, wo2x)
    w_o = w_o.reshape(D, D)

    residual, normed = attention_out(mixed, sent, w_o, inputs, gain, shift)
    normed_x = x_swap(normed)
    hid, gb, up_cols, branch, gn = feed_forward(normed, cotangent, up_shift, ffn_own, ffn_par, F32)

    other = c_swap(jnp.stack([inputs, inputs_x]))

    def memory_moves(index, ins, outs):
        me = index[0]
        yield ins[0], outs[0].at[me]
        yield ins[1], outs[0].at[me ^ 2]
        yield ins[2].at[0], outs[0].at[me ^ 1]
        yield ins[2].at[1], outs[0].at[me ^ 3]

    (new_memory,) = copies(memory_moves, [(seqs, SEG, D)], h1, inputs, inputs_x, other)
    new_compressed = compress(h1, memory, compressed, comp_w, comp_bias)

    hid_x, gb_x, up_cols_x, branch_x, gn_x = feed_forward(normed_x, cot_x, up_shift, ffn_own, ffn_par, BF)
    gn_x = x_swap(gn_x)
    branch_x = x_swap(branch_x)
    output = (residual + branch + branch_x.astype(F32) + down_shift).astype(BF)

    acts = ((normed, normed_x), (cotangent, cot_x), (gb, gb_x), (hid, hid_x))
    from_par = c_swap(ffn_grads(1, n_dp, *acts))
    ffn_sum = ring_scatter(ffn_grads(0, n_dp, *acts, from_par), d, n_dp)
    grad_up, grad_down = ffn_sum[0], ffn_sum[1].T

    grad_residual, do, do_x, sums, g_out = norm_back(h1, residual, gn, gn_x, cotangent, gain, mixed, sent, w_o)
    do_x = x_swap(do_x)
    g_out = g_out.reshape(n_dp, 2, 2, out_rows, D)
    cc, xx = h % 2, h // 2
    g_out = (pick(g_out, cc, 2).astype(F32) + c_swap(pick(g_out, 1 - cc, 2)).astype(F32)).astype(BF)
    g_out = (pick(g_out, xx, 1).astype(F32) + x_swap(pick(g_out, 1 - xx, 1)).astype(F32)).astype(BF)
    grad_out = lax.psum_scatter(g_out.reshape(n_dp * out_rows, D), "dp", scatter_dimension=0, tiled=True).astype(F32)

    dq, dkv, q_cols = attend_back(0, slopes, q, kv, near, far[0], mixed, lse, do)
    term = token_term(dq, dkv, w_own, w_par, grad_residual)
    dq_x, dkv_x, q_cols_x = attend_back(1, slopes, q, kv, near, far[1], mixed_x, lse_x, do_x)
    term_x = x_swap(token_term(dq_x, dkv_x, w_own, w_par))
    grad_input = term + term_x.astype(F32)

    lane = jnp.arange(4)[:, None]

    def place(a):
        a = a.reshape(2, 1, -1)
        return jnp.where(lane == h, a[0], 0.0) + jnp.where(lane == h ^ 1, a[1], 0.0)

    tiny = jnp.concatenate([
        place(q_cols + q_cols_x).reshape(-1, share),
        sums[0].reshape(-1, share),
        sums[1].reshape(-1, share),
        sums[2].reshape(-1, share),
        place(up_cols + up_cols_x).reshape(-1, up_share),
    ], axis=1)
    tiny = tiny + x_swap(tiny)
    tiny = tiny + c_swap(tiny)
    tiny = jnp.pad(tiny.astype(BF).reshape(n_dp, 4, values), ((0, 0), (0, 12), (0, 6 * HD - values)))

    work = (ids, compressed, memory, inputs, inputs_x, (dkv, dkv_x), (dq, dq_x))
    from_par = c_swap(weight_grads(1, n_dp, *work))
    g_sum = ring_scatter(weight_grads(0, n_dp, *work, from_par, tiny), d, n_dp)
    tiny = pick(g_sum[rows:], h, 0)
    g_sum = g_sum[:rows]
    grad_key = jnp.concatenate([g_sum[:, :HD], g_sum[:, 2 * HD:3 * HD]], axis=1)
    grad_value = jnp.concatenate([g_sum[:, HD:2 * HD], g_sum[:, 3 * HD:4 * HD]], axis=1)
    grad_query = g_sum[:, 4 * HD:]

    return (
        output,
        grad_input,
        grad_query,
        grad_key,
        grad_value,
        tiny[:share],
        grad_out,
        tiny[share:2 * share],
        tiny[2 * share:3 * share],
        grad_up,
        tiny[4 * share:values],
        grad_down,
        tiny[3 * share:4 * share],
        new_memory,
        new_compressed,
    )


def solution(mesh):
    both = ("dp", "head")
    in_specs = (
        P(both, None),
        P("dp", None, None),
        P("dp", None, None),
        P("dp", None),
        P("dp", None),
        P("dp", "head"),
        P("dp", "head"),
        P("dp", "head"),
        P(both),
        P(both, None),
        P(both),
        P(both),
        P("dp", "head"),
        P(both),
        P("head", "dp"),
        P(both),
        P(None, "dp", "head"),
        P("head"),
        P(both, None),
    )
    out_specs = (
        P(both, None),
        P(both, None),
        P("dp", "head"),
        P("dp", "head"),
        P("dp", "head"),
        P(both),
        P(both, None),
        P(both),
        P(both),
        P("dp", "head"),
        P(both),
        P("head", "dp"),
        P(both),
        P("dp", None, None),
        P("dp", None, "head"),
    )
    return jax.shard_map(per_device, mesh=mesh, in_specs=in_specs, out_specs=out_specs, check_vma=False)
```

time: 654 us -> 495 us (0.76)
  matrix products: 133 us -> 0 us
  Pallas kernels: 57.5 us -> 183 us
  blocking collectives: 87.9 us -> 0 us
  waiting for transfers between devices: 215 us -> 172 us
  local copies, waits for them, and re-layouts: 69.1 us -> 31.6 us
  starting transfers between devices: 18.8 us -> 51.3 us
  other arithmetic: 51.9 us -> 36.2 us
    dot_general x52 -> x0, matrix products: 133 us -> none  [the longest x18 52.5 us: nn(): return jnp.dot(a, b, preferred_element_type=F32)]
    pallas_call x8 -> x20, Pallas kernels: 57.5 us -> 183 us  [the longest x2 32.2 us: feed_forward(): pl.pallas_call(ffn_kernel, grid=(2 * n,), in_specs=[whole(SEG, D), whole(...]
    unnamed x10 -> x2, waiting for transfers between devices: 110 us -> 0.03 us
    all_gather x2 -> x0, blocking collectives: 87.9 us -> none  [the longest x1 55 us: per_device(): lax.all_gather(small, ('dp', 'head'), axis=0, tiled=True).astype(F32)]
    ppermute x6 -> x28, waiting for transfers between devices: 17.3 us -> 77.9 us  [the longest x8 23.9 us: ring_gather(): f = lax.ppermute(f, 'dp', ahead)]
    ppermute x6 -> x28, starting transfers between devices: 3.63 us -> 36.3 us  [the longest x8 17.5 us: ring_gather(): f = lax.ppermute(f, 'dp', ahead)]
    reduce_scatter x1, waiting for transfers between devices: 0.01 us -> 19.9 us  [per_device(): lax.psum_scatter(g_out.reshape(n_dp * out_rows, D), 'dp', scatter_dimensi...]
    gather x4 -> x1, local copies, waits for them, and re-layouts: 15.9 us -> 0.57 us  [per_device(): small = jnp.take(small, h ^ jnp.arange(4), axis=0, mode='clip')]
  transfers between devices with their start and end apart: 37 -> 51, of which waited for: 13 -> 19; matrix products, arithmetic and copies ran while one was open for 34% -> 11% of each run, Pallas kernels for 9% -> 34%
where the time goes in v2:
time: 495 us; the launch traced here: 489 us
  Pallas kernels  183 us (37%)
  waiting for transfers between devices  172 us (35%)
  starting transfers between devices  51.3 us (10%)
  other arithmetic  36.2 us (7%)
  local copies, waits for them, and re-layouts  31.6 us (6%)
  between operations  15.2 us (3%)
    ppermute x12, waiting for transfers between devices, x_swap(): return lax.ppermute(a, 'head', [(i, i ^ 2) for i in range(4)])  73.8 us
    pallas_call x2, Pallas kernels, feed_forward(): pl.pallas_call(ffn_kernel, grid=(2 * n,), in_specs=[whole(SEG, D), whole(...  32.2 us
    pallas_call x2, Pallas kernels, attend_back(): pl.pallas_call(bwd_kernel, grid=(4,), in_specs=[smem_spec, pl.BlockSpec((...  25.8 us
    ppermute x8, waiting for transfers between devices, ring_gather(): f = lax.ppermute(f, 'dp', ahead)  23.9 us
    ppermute x6, waiting for transfers between devices, ring_gather(): b = lax.ppermute(b, 'dp', back)  23.8 us
    pallas_call x2, Pallas kernels, weight_grads(): pl.pallas_call(weight_grad_kernel, grid_spec=pltpu.PrefetchScalarGridSpec...  22.2 us
    reduce_scatter x1, waiting for transfers between devices, per_device(): lax.psum_scatter(g_out.reshape(n_dp * out_rows, D), 'dp', scatter_dimensi...  19.9 us
    pallas_call x2, Pallas kernels, ffn_grads(): pl.pallas_call(ffn_grad_kernel, grid=(2, n), in_specs=[tokens] * 4 + [ear...  19.8 us
  transfers between devices with their start and end apart: 51, of which 19 were waited for; matrix products, arithmetic and copies ran while one was open for 11% of the time, Pallas kernels for 34%

profile of v2, /device:TPU:0, one launch (start us, length us, event | category | flops | bytes accessed | tf_op | source)
XLA Modules:
  0.0 489.3 jit_solution(11594002045493586703)
XLA Ops:
  25.3 12.0 %collective-permute-done.2 = bf16[2,256]{1,0:T(2,128)(2,1)S(1)} collective-permute-done((bf16[2,256]{1,0:T(2,128)(2,1)S(1)}, bf16[2,256]{1,0:T(2,128)(2,1)S(1)}, u32[]{:S(2)}, u32[]{:S(2)}) %collective-permute-start.2) | collective-permute-done | bytes 1056 | tf_op jit(solution)/shard_map/ppermute | solution.py:36
  51.7 6.6 %collective-permute-done.5.refs_3_ = bf16[144,768]{1,0:T(8,128)(2,1)S(1)} collective-permute-done((bf16[144,768]{1,0:T(8,128)(2,1)S(1)}, bf16[144,768]{1,0:T(8,128)(2,1)S(1)}, u32[]{:S(2)}, u32[]{:S(2)}) %collective-permute-start.5) | collective-permute-done | bytes 221216 | tf_op jit(solution)/shard_map/ppermute | solution.py:112
  94.9 11.8 %collective-permute-done.17.refs_4_ = bf16[256,1024]{1,0:T(8,128)(2,1)} collective-permute-done((bf16[256,1024]{1,0:T(8,128)(2,1)}, bf16[256,1024]{1,0:T(8,128)(2,1)}, u32[]{:S(2)}, u32[]{:S(2)}) %collective-permute-start.17) | collective-permute-done | bytes 524320 | tf_op jit(solution)/shard_map/ppermute | solution.py:115
  113.9 6.7 %collective-permute-done.19.refs_6_ = bf16[256,1024]{1,0:T(8,128)(2,1)} collective-permute-done((bf16[256,1024]{1,0:T(8,128)(2,1)}, bf16[256,1024]{1,0:T(8,128)(2,1)}, u32[]{:S(2)}, u32[]{:S(2)}) %collective-permute-start.19) | collective-permute-done | bytes 524320 | tf_op jit(solution)/shard_map/ppermute | solution.py:115
  127.7 14.2 %shard_map.308 = (bf16[2,1536,1024]{2,1,0:T(8,128)(2,1)}, bf16[2,512,512]{2,1,0:T(8,128)(2,1)}) custom-call(s32[2]{0:T(128)} %pad_add_fusion.ids_ref, bf16[4,512,1024]{2,1,0:T(8,128)(2,1)} %compressed_ref.1, bf16[4,512,1024]{2,1,0:T(8,128)(2,1)} %memory_ref.1, bf16[512,1024]{1,0:T(8,128)(2,1)} %refs_0_.1, bf16[512,1024]{1,0:T(8,128)(2,1)} %copy-done.2, ...), custom_call_target="tpu_custom_call" | custom-call | flops 13200000000 | bytes 1048576 | tf_op jit(solution)/shard_map/pallas_call | solution.py:232
  141.9 9.4 %shard_map.309 = (bf16[512,512]{1,0:T(8,128)(2,1)}, f32[4,1,512]{2,1,0:T(1,128)}) custom-call(f32[4]{0:T(128)} %fusion.20.slope_ref, bf16[2,512,512]{2,1,0:T(8,128)(2,1)} %get-tuple-element.48.q_ref, bf16[2,1536,1024]{2,1,0:T(8,128)(2,1)} %get-tuple-element.49.kv_ref, f32[1024,512]{1,0:T(8,128)} %log-plus-one_select_fusion.near_ref, ...), custom_call_target="tpu_custom_call" | custom-call | flops 13200000000 | bytes 1048576 | tf_op jit(solution)/shard_map/pallas_call | solution.py:174
  153.7 9.4 %shard_map.310 = (bf16[512,512]{1,0:T(8,128)(2,1)}, f32[4,1,512]{2,1,0:T(1,128)}) custom-call(f32[4]{0:T(128)} %fusion.20.slope_ref, bf16[2,512,512]{2,1,0:T(8,128)(2,1)} %get-tuple-element.48.q_ref, bf16[2,1536,1024]{2,1,0:T(8,128)(2,1)} %get-tuple-element.49.kv_ref, f32[1024,512]{1,0:T(8,128)} %log-plus-one_select_fusion.near_ref, ...), custom_call_target="tpu_custom_call" | custom-call | flops 13200000000 | bytes 1048576 | tf_op jit(solution)/shard_map/pallas_call | solution.py:174
  173.3 8.9 %shard_map.326 = bf16[4,512,256]{2,1,0:T(8,128)(2,1)} custom-call(s32[1]{0:T(128)} %bitcast.index_ref.h_ref, bf16[4,512,1024]{2,1,0:T(8,128)(2,1)} %memory_ref.1, bf16[4,512,1024]{2,1,0:T(8,128)(2,1)} %compressed_ref.1, bf16[8,3,128,256]{3,2,1,0:T(8,128)(2,1)} %bitcast.128, bf16[1,256]{1,0:T(2,128)(2,1)} %reshape.214.bias_ref), custom_call_target="tpu_custom_call" | custom-call | flops 8800000000 | bytes 1048576 | tf_op jit(solution)/shard_map/pallas_call | solution.py:578
  182.1 17.6 %collective-permute-done.13.refs_1_ = bf16[2,8,32,1024]{3,2,1,0:T(8,128)(2,1)S(1)} collective-permute-done((bf16[2,8,32,1024]{3,2,1,0:T(8,128)(2,1)S(1)}, bf16[2,8,32,1024]{3,2,1,0:T(8,128)(2,1)S(1)}, u32[]{:S(2)}, u32[]{:S(2)}) %collective-permute-start.13) | collective-permute-done | bytes 1048608 | tf_op jit(solution)/shard_map/ppermute | solution.py:36
  209.9 16.4 %shard_map.314 = (bf16[512,2048]{1,0:T(8,128)(2,1)}, bf16[512,2048]{1,0:T(8,128)(2,1)}, f32[1,2048]{1,0:T(1,128)}, f32[512,1024]{1,0:T(8,128)}, f32[512,1024]{1,0:T(8,128)}) custom-call(bf16[512,1024]{1,0:T(8,128)(2,1)} %get-tuple-element.53.norm_ref.n0, bf16[512,1024]{1,0:T(8,128)(2,1)} %c0.3, f32[1,2048]{1,0:T(1,128)} %bitcast.137, ...), custom_call_target="tpu_custom_call" | custom-call | flops 17600000000 | bytes 1048576 | tf_op jit(solution)/shard_map/pallas_call | solution.py:322
  226.3 6.5 %collective-permute-done.22.norm_ref.n1 = bf16[512,1024]{1,0:T(8,128)(2,1)S(1)} collective-permute-done((bf16[512,1024]{1,0:T(8,128)(2,1)}, bf16[512,1024]{1,0:T(8,128)(2,1)S(1)}, u32[]{:S(2)}, u32[]{:S(2)}) %collective-permute-start.22) | collective-permute-done | bytes 1048608 | tf_op jit(solution)/shard_map/ppermute | solution.py:36
  233.8 15.8 %shard_map.315 = (bf16[512,2048]{1,0:T(8,128)(2,1)}, bf16[512,2048]{1,0:T(8,128)(2,1)}, f32[1,2048]{1,0:T(1,128)}, bf16[512,1024]{1,0:T(8,128)(2,1)}, bf16[512,1024]{1,0:T(8,128)(2,1)}) custom-call(bf16[512,1024]{1,0:T(8,128)(2,1)} %copy-done.19, bf16[512,1024]{1,0:T(8,128)(2,1)} %collective-permute-done.23.cot_ref.c1, f32[1,2048]{1,0:T(1,128)} %bitcast.138, ...), custom_call_target="tpu_custom_call" | custom-call | flops 17600000000 | bytes 1048576 | tf_op jit(solution)/shard_map/pallas_call | solution.py:322
  251.7 9.6 %shard_map.323 = bf16[8,2,128,1024]{3,2,1,0:T(8,128)(2,1)} custom-call(bf16[512,1024]{1,0:T(8,128)(2,1)} %get-tuple-element.53.norm_ref.n0, bf16[512,1024]{1,0:T(8,128)(2,1)} %copy-done.19, bf16[512,1024]{1,0:T(8,128)(2,1)} %c0.3, bf16[512,1024]{1,0:T(8,128)(2,1)} %collective-permute-done.23.cot_ref.c1, bf16[512,2048]{1,0:T(8,128)(2,1)} %get-tuple-element.73.gb0, ...), custom_call_target="tpu_custom_call" | custom-call | flops 7699999744 | bytes 1048576 | tf_op jit(solution)/shard_map/pallas_call | solution.py:362
  261.4 34.3 %collective-permute-done.25.gnx_ref = bf16[512,1024]{1,0:T(8,128)(2,1)S(1)} collective-permute-done((bf16[512,1024]{1,0:T(8,128)(2,1)}, bf16[512,1024]{1,0:T(8,128)(2,1)S(1)}, u32[]{:S(2)}, u32[]{:S(2)}) %collective-permute-start.25) | collective-permute-done | bytes 1048608 | tf_op jit(solution)/shard_map/ppermute | solution.py:36
  296.7 9.7 %shard_map.316 = (f32[512,1024]{1,0:T(8,128)}, bf16[512,512]{1,0:T(8,128)(2,1)}, bf16[512,512]{1,0:T(8,128)(2,1)}, f32[3,1024]{1,0:T(4,128)}, bf16[4,256,1024]{2,1,0:T(8,128)(2,1)}) custom-call(s32[1]{0:T(128)} %bitcast.index_ref.h_ref, f32[512,1024]{1,0:T(8,128)} %get-tuple-element.52.residual_ref, f32[512,1024]{1,0:T(8,128)} %get-tuple-element.57.gn_ref, ...), custom_call_target="tpu_custom_call" | custom-call | flops 7699999744 | bytes 1048576 | tf_op jit(solution)/shard_map/pallas_call | solution.py:413
  310.4 13.0 %shard_map.317 = (bf16[512,512]{1,0:T(8,128)(2,1)}, bf16[1536,1024]{1,0:T(8,128)(2,1)}, f32[1,512]{1,0:T(1,128)}) custom-call(f32[4]{0:T(128)} %fusion.20.slope_ref, bf16[2,512,512]{2,1,0:T(8,128)(2,1)} %get-tuple-element.48.q_ref, bf16[2,1536,1024]{2,1,0:T(8,128)(2,1)} %get-tuple-element.49.kv_ref, f32[1024,512]{1,0:T(8,128)} %log-plus-one_select_fusion.near_ref, ...), custom_call_target="tpu_custom_call" | custom-call | flops 17600000000 | bytes 1048576 | tf_op jit(solution)/shard_map/pallas_call | solution.py:193
  324.2 12.7 %shard_map.319 = (bf16[512,512]{1,0:T(8,128)(2,1)}, bf16[1536,1024]{1,0:T(8,128)(2,1)}, f32[1,512]{1,0:T(1,128)}) custom-call(f32[4]{0:T(128)} %fusion.20.slope_ref, bf16[2,512,512]{2,1,0:T(8,128)(2,1)} %get-tuple-element.48.q_ref, bf16[2,1536,1024]{2,1,0:T(8,128)(2,1)} %get-tuple-element.49.kv_ref, f32[1024,512]{1,0:T(8,128)} %log-plus-one_select_fusion.near_ref, ...), custom_call_target="tpu_custom_call" | custom-call | flops 17600000000 | bytes 1048576 | tf_op jit(solution)/shard_map/pallas_call | solution.py:193
  337.0 10.6 %shard_map.321 = bf16[8,128,768]{2,1,0:T(8,128)(2,1)} custom-call(s32[2]{0:T(128)} %pad_add_fusion.ids_ref, bf16[4,512,1024]{2,1,0:T(8,128)(2,1)} %compressed_ref.1, bf16[4,512,1024]{2,1,0:T(8,128)(2,1)} %memory_ref.1, bf16[512,1024]{1,0:T(8,128)(2,1)} %refs_0_.1, bf16[512,1024]{1,0:T(8,128)(2,1)} %copy-done.2, ...), custom_call_target="tpu_custom_call" | custom-call | flops 7699999744 | bytes 1048576 | tf_op jit(solution)/shard_map/pallas_call | solution.py:489
  364.3 11.5 %shard_map.322 = bf16[8,144,768]{2,1,0:T(8,128)(2,1)} custom-call(s32[2]{0:T(128)} %pad_add_fusion.ids_ref, bf16[4,512,1024]{2,1,0:T(8,128)(2,1)} %compressed_ref.1, bf16[4,512,1024]{2,1,0:T(8,128)(2,1)} %memory_ref.1, bf16[512,1024]{1,0:T(8,128)(2,1)} %refs_0_.1, bf16[512,1024]{1,0:T(8,128)(2,1)} %copy-done.2, ...), custom_call_target="tpu_custom_call" | custom-call | flops 7699999744 | bytes 1048576 | tf_op jit(solution)/shard_map/pallas_call | solution.py:489
  379.0 10.2 %shard_map.324 = bf16[8,2,128,1024]{3,2,1,0:T(8,128)(2,1)} custom-call(bf16[512,1024]{1,0:T(8,128)(2,1)} %get-tuple-element.53.norm_ref.n0, bf16[512,1024]{1,0:T(8,128)(2,1)} %copy-done.19, bf16[512,1024]{1,0:T(8,128)(2,1)} %c0.3, bf16[512,1024]{1,0:T(8,128)(2,1)} %collective-permute-done.23.cot_ref.c1, bf16[512,2048]{1,0:T(8,128)(2,1)} %get-tuple-element.73.gb0, ...), custom_call_target="tpu_custom_call" | custom-call | flops 7699999744 | bytes 1048576 | tf_op jit(solution)/shard_map/pallas_call | solution.py:362
  398.1 12.3 %collective-permute-done.32 = bf16[144,768]{1,0:T(8,128)(2,1)} collective-permute-done((bf16[144,768]{1,0:T(8,128)(2,1)}, bf16[144,768]{1,0:T(8,128)(2,1)}, u32[]{:S(2)}, u32[]{:S(2)}) %collective-permute-start.32) | collective-permute-done | bytes 221216 | tf_op jit(solution)/shard_map/ppermute | solution.py:140
  425.7 8.1 %collective-permute-done.45 = bf16[2,128,1024]{2,1,0:T(8,128)(2,1)S(1)} collective-permute-done((bf16[2,128,1024]{2,1,0:T(8,128)(2,1)}, bf16[2,128,1024]{2,1,0:T(8,128)(2,1)S(1)}, u32[]{:S(2)}, u32[]{:S(2)}) %collective-permute-start.45) | collective-permute-done | bytes 524320 | tf_op jit(solution)/shard_map/ppermute | solution.py:144
  440.2 19.9 %reduce-scatter.2.cloned.1.call-done = bf16[32,1024]{1,0:T(8,128)(2,1)} async-done(((bf16[256,1024]{1,0:T(8,128)(2,1)}), bf16[32,1024]{1,0:T(8,128)(2,1)}) %reduce-scatter.2.cloned.1.call-update) | async-done | bytes 65552 | tf_op jit(solution)/shard_map/reduce_scatter | solution.py:736
  470.1 7.8 %collective-permute-done.47 = bf16[2,128,1024]{2,1,0:T(8,128)(2,1)S(1)} collective-permute-done((bf16[2,128,1024]{2,1,0:T(8,128)(2,1)S(1)}, bf16[2,128,1024]{2,1,0:T(8,128)(2,1)S(1)}, u32[]{:S(2)}, u32[]{:S(2)}) %collective-permute-start.47) | collective-permute-done | bytes 524320 | tf_op jit(solution)/shard_map/ppermute | solution.py:144
  (248 shorter events, 179.2 us)
Async XLA Ops:
  7.2 144.1 %all-gather.2.cloned.1.call-start = ((), (), s32[]{:S(2)}) async-start(), calls=%async_computation.1 | async-start | bytes 2359296 | tf_op jit(solution)/shard_map/all_gather | solution.py:645
  9.4 62.9 %collective-permute-start.14 = (bf16[256,1024]{1,0:T(8,128)(2,1)S(1)}, bf16[256,1024]{1,0:T(8,128)(2,1)S(1)}, u32[]{:S(2)}, u32[]{:S(2)}) collective-permute-start(bf16[256,1024]{1,0:T(8,128)(2,1)S(1)} %pad_maximum_fusion.2.refs_0_), channel_id=1, source_target_pairs={{0,8},{8,16},{16,24},{24,28},{28,20},{20,12},{12,4},{4,0},{1,9},{9... | collective-permute-start | bytes 1572872 | tf_op jit(solution)/shard_map/ppermute | solution.py:112
  12.5 79.6 %collective-permute-start.15 = (bf16[256,1024]{1,0:T(8,128)(2,1)S(1)}, bf16[256,1024]{1,0:T(8,128)(2,1)}, u32[]{:S(2)}, u32[]{:S(2)}) collective-permute-start(bf16[256,1024]{1,0:T(8,128)(2,1)S(1)} %pad_maximum_fusion.2.refs_0_), channel_id=1, source_target_pairs={{8,0},{16,8},{24,16},{28,24},{20,28},{12,20},{4,12},{0,4},{9,1},{1... | collective-permute-start | bytes 1572872 | tf_op jit(solution)/shard_map/ppermute | solution.py:115
  12.5 99.7 %collective-permute-start = (bf16[512,1024]{1,0:T(8,128)(2,1)}, bf16[512,1024]{1,0:T(8,128)(2,1)S(1)}, u32[]{:S(2)}, u32[]{:S(2)}) collective-permute-start(bf16[512,1024]{1,0:T(8,128)(2,1)} %refs_0_.1), channel_id=1, source_target_pairs={{0,2},{1,3},{2,0},{3,1},{4,6},{5,7},{6,4},{7,5},{8,10},{9,11},{10,... | collective-permute-start | bytes 3145736 | tf_op jit(solution)/shard_map/ppermute | solution.py:36
  22.5 437.6 %reduce-scatter.2.cloned.1.call-start = ((), (), s32[]{:S(2)}) async-start(), calls=%async_computation.2 | async-start | bytes 589824 | tf_op jit(solution)/shard_map/reduce_scatter | solution.py:736
  72.3 21.8 %collective-permute-start.16 = (bf16[256,1024]{1,0:T(8,128)(2,1)S(1)}, bf16[256,1024]{1,0:T(8,128)(2,1)}, u32[]{:S(2)}, u32[]{:S(2)}) collective-permute-start(bf16[256,1024]{1,0:T(8,128)(2,1)S(1)} %collective-permute-done.14.refs_1_), channel_id=1, source_target_pairs={{0,8},{8,16},{16,24},{24,28},{28,20},{20,12},{12,4},{4,0},{1,9},{9... | collective-permute-start | bytes 1572872 | tf_op jit(solution)/shard_map/ppermute | solution.py:112
  78.3 148.0 %collective-permute-start.23 = (bf16[512,1024]{1,0:T(8,128)(2,1)}, bf16[512,1024]{1,0:T(8,128)(2,1)}, u32[]{:S(2)}, u32[]{:S(2)}) collective-permute-start(bf16[512,1024]{1,0:T(8,128)(2,1)} %c0.3), channel_id=1, source_target_pairs={{0,2},{1,3},{2,0},{3,1},{4,6},{5,7},{6,4},{7,5},{8,10},{9,11},{10,... | collective-permute-start | bytes 3145736 | tf_op jit(solution)/shard_map/ppermute | solution.py:36
  90.5 37.2 %collective-permute-start.10 = (bf16[1024,768]{1,0:T(8,128)(2,1)}, bf16[1024,768]{1,0:T(8,128)(2,1)}, u32[]{:S(2)}, u32[]{:S(2)}) collective-permute-start(bf16[1024,768]{1,0:T(8,128)(2,1)} %get-tuple-element.46.w_own_ref), channel_id=1, source_target_pairs={{0,1},{1,0},{2,3},{3,2},{4,5},{5,4},{6,7},{7,6},{8,9},{9,8},{10,11... | collective-permute-start | bytes 4718600 | tf_op jit(solution)/shard_map/ppermute | solution.py:40
  113.9 53.9 %collective-permute-start.48 = (bf16[2,512,1024]{2,1,0:T(8,128)(2,1)}, bf16[2,512,1024]{2,1,0:T(8,128)(2,1)}, u32[]{:S(2)}, u32[]{:S(2)}) collective-permute-start(bf16[2,512,1024]{2,1,0:T(8,128)(2,1)} %pad_maximum_fusion), channel_id=1, source_target_pairs={{0,1},{1,0},{2,3},{3,2},{4,5},{5,4},{6,7},{7,6},{8,9},{9,8},{10,11... | collective-permute-start | bytes 6291464 | tf_op jit(solution)/shard_map/ppermute | solution.py:40
  127.6 82.3 %collective-permute-start.21 = (bf16[2048,1024]{1,0:T(8,128)(2,1)}, bf16[2048,1024]{1,0:T(8,128)(2,1)}, u32[]{:S(2)}, u32[]{:S(2)}) collective-permute-start(bf16[2048,1024]{1,0:T(8,128)(2,1)} %shard_map.313.up0.down0), channel_id=1, source_target_pairs={{0,1},{1,0},{2,3},{3,2},{4,5},{5,4},{6,7},{7,6},{8,9},{9,8},{10,11... | collective-permute-start | bytes 12582920 | tf_op jit(solution)/shard_map/ppermute | solution.py:40
  163.1 39.9 %collective-permute-start.11 = (bf16[512,512]{1,0:T(8,128)(2,1)}, bf16[512,512]{1,0:T(8,128)(2,1)}, u32[]{:S(2)}, u32[]{:S(2)}) collective-permute-start(bf16[512,512]{1,0:T(8,128)(2,1)} %get-tuple-element.51.mixed_ref), channel_id=1, source_target_pairs={{0,2},{1,3},{2,0},{3,1},{4,6},{5,7},{6,4},{7,5},{8,10},{9,11},{10,... | collective-permute-start | bytes 1572872 | tf_op jit(solution)/shard_map/ppermute | solution.py:36
  167.1 32.6 %collective-permute-start.13 = (bf16[2,8,32,1024]{3,2,1,0:T(8,128)(2,1)S(1)}, bf16[2,8,32,1024]{3,2,1,0:T(8,128)(2,1)S(1)}, u32[]{:S(2)}, u32[]{:S(2)}) collective-permute-start(bf16[2,8,32,1024]{3,2,1,0:T(8,128)(2,1)S(1)} %pad_maximum_fusion.1.refs_0_), channel_id=1, source_target_pairs={{0,2},{1,3},{2,0},{3,1},{4,6},{5,7},{6,4},{7,5},{8,10},{9,11},{10,... | collective-permute-start | bytes 3145736 | tf_op jit(solution)/shard_map/ppermute | solution.py:36
  208.4 24.5 %collective-permute-start.22 = (bf16[512,1024]{1,0:T(8,128)(2,1)}, bf16[512,1024]{1,0:T(8,128)(2,1)S(1)}, u32[]{:S(2)}, u32[]{:S(2)}) collective-permute-start(bf16[512,1024]{1,0:T(8,128)(2,1)} %get-tuple-element.53.norm_ref.n0), channel_id=1, source_target_pairs={{0,2},{1,3},{2,0},{3,1},{4,6},{5,7},{6,4},{7,5},{8,10},{9,11},{10,... | collective-permute-start | bytes 3145736 | tf_op jit(solution)/shard_map/ppermute | solution.py:36
  249.6 166.1 %collective-permute-start.24 = (bf16[512,1024]{1,0:T(8,128)(2,1)}, bf16[512,1024]{1,0:T(8,128)(2,1)}, u32[]{:S(2)}, u32[]{:S(2)}) collective-permute-start(bf16[512,1024]{1,0:T(8,128)(2,1)} %get-tuple-element.55), channel_id=1, source_target_pairs={{0,2},{1,3},{2,0},{3,1},{4,6},{5,7},{6,4},{7,5},{8,10},{9,11},{10,... | collective-permute-start | bytes 3145736 | tf_op jit(solution)/shard_map/ppermute | solution.py:36
  251.2 44.5 %collective-permute-start.25 = (bf16[512,1024]{1,0:T(8,128)(2,1)}, bf16[512,1024]{1,0:T(8,128)(2,1)S(1)}, u32[]{:S(2)}, u32[]{:S(2)}) collective-permute-start(bf16[512,1024]{1,0:T(8,128)(2,1)} %get-tuple-element.58), channel_id=1, source_target_pairs={{0,2},{1,3},{2,0},{3,1},{4,6},{5,7},{6,4},{7,5},{8,10},{9,11},{10,... | collective-permute-start | bytes 3145736 | tf_op jit(solution)/shard_map/ppermute | solution.py:36
  261.3 115.9 %collective-permute-start.40 = (bf16[8,2,128,1024]{3,2,1,0:T(8,128)(2,1)}, bf16[8,2,128,1024]{3,2,1,0:T(8,128)(2,1)}, u32[]{:S(2)}, u32[]{:S(2)}) collective-permute-start(bf16[8,2,128,1024]{3,2,1,0:T(8,128)(2,1)} %shard_map.323), channel_id=1, source_target_pairs={{0,1},{1,0},{2,3},{3,2},{4,5},{5,4},{6,7},{7,6},{8,9},{9,8},{10,11... | collective-permute-start | bytes 12582920 | tf_op jit(solution)/shard_map/ppermute | solution.py:40
  310.3 51.7 %collective-permute-start.38 = (bf16[8,2,32,1024]{3,2,1,0:T(8,128)(2,1)S(1)}, bf16[8,2,32,1024]{3,2,1,0:T(8,128)(2,1)S(1)}, u32[]{:S(2)}, u32[]{:S(2)}) collective-permute-start(bf16[8,2,32,1024]{3,2,1,0:T(8,128)(2,1)S(1)} %dynamic-slice_bitcast_fusion), channel_id=1, source_target_pairs={{0,1},{1,0},{2,3},{3,2},{4,5},{5,4},{6,7},{7,6},{8,9},{9,8},{10,11... | collective-permute-start | bytes 3145736 | tf_op jit(solution)/shard_map/ppermute | solution.py:40
  359.8 78.7 %collective-permute-start.27 = (bf16[512,1024]{1,0:T(8,128)(2,1)}, bf16[512,1024]{1,0:T(8,128)(2,1)S(1)}, u32[]{:S(2)}, u32[]{:S(2)}) collective-permute-start(bf16[512,1024]{1,0:T(8,128)(2,1)} %shard_map.320), channel_id=1, source_target_pairs={{0,2},{1,3},{2,0},{3,1},{4,6},{5,7},{6,4},{7,5},{8,10},{9,11},{10,... | collective-permute-start | bytes 3145736 | tf_op jit(solution)/shard_map/ppermute | solution.py:36
  363.7 33.1 %collective-permute-start.39 = (bf16[8,32,1024]{2,1,0:T(8,128)(2,1)S(1)}, bf16[8,32,1024]{2,1,0:T(8,128)(2,1)S(1)}, u32[]{:S(2)}, u32[]{:S(2)}) collective-permute-start(bf16[8,32,1024]{2,1,0:T(8,128)(2,1)S(1)} %dynamic-slice_bitcast_fusion.3), channel_id=1, source_target_pairs={{0,2},{1,3},{2,0},{3,1},{4,6},{5,7},{6,4},{7,5},{8,10},{9,11},{10,... | collective-permute-start | bytes 1572872 | tf_op jit(solution)/shard_map/ppermute | solution.py:36
  391.4 22.4 %collective-permute-start.41 = (bf16[2,128,1024]{2,1,0:T(8,128)(2,1)}, bf16[2,128,1024]{2,1,0:T(8,128)(2,1)}, u32[]{:S(2)}, u32[]{:S(2)}) collective-permute-start(bf16[2,128,1024]{2,1,0:T(8,128)(2,1)} %get-tuple-element.103), channel_id=1, source_target_pairs={{0,8},{8,16},{16,24},{24,28},{28,20},{20,12},{12,4},{4,0},{1,9},{9... | collective-permute-start | bytes 1572872 | tf_op jit(solution)/shard_map/ppermute | solution.py:140
  423.7 37.9 %collective-permute-start.37 = (bf16[144,768]{1,0:T(8,128)(2,1)}, bf16[144,768]{1,0:T(8,128)(2,1)}, u32[]{:S(2)}, u32[]{:S(2)}) collective-permute-start(bf16[144,768]{1,0:T(8,128)(2,1)} %get-tuple-element.106), channel_id=1, source_target_pairs={{8,0},{16,8},{24,16},{28,24},{20,28},{12,20},{4,12},{0,4},{9,1},{1... | collective-permute-start | bytes 663560 | tf_op jit(solution)/shard_map/ppermute | solution.py:144
  424.4 37.2 %collective-permute-start.34 = (bf16[144,768]{1,0:T(8,128)(2,1)S(1)}, bf16[144,768]{1,0:T(8,128)(2,1)}, u32[]{:S(2)}, u32[]{:S(2)}) collective-permute-start(bf16[144,768]{1,0:T(8,128)(2,1)S(1)} %get-tuple-element.105), channel_id=1, source_target_pairs={{0,8},{8,16},{16,24},{24,28},{28,20},{20,12},{12,4},{4,0},{1,9},{9... | collective-permute-start | bytes 663560 | tf_op jit(solution)/shard_map/ppermute | solution.py:140
  436.4 27.7 %collective-permute-start.43 = (bf16[2,128,1024]{2,1,0:T(8,128)(2,1)}, bf16[2,128,1024]{2,1,0:T(8,128)(2,1)}, u32[]{:S(2)}, u32[]{:S(2)}) collective-permute-start(bf16[2,128,1024]{2,1,0:T(8,128)(2,1)} %get-tuple-element.101), channel_id=1, source_target_pairs={{0,8},{8,16},{16,24},{24,28},{28,20},{20,12},{12,4},{4,0},{1,9},{9... | collective-permute-start | bytes 1572872 | tf_op jit(solution)/shard_map/ppermute | solution.py:140
  436.8 27.3 %collective-permute-start.46 = (bf16[2,128,1024]{2,1,0:T(8,128)(2,1)}, bf16[2,128,1024]{2,1,0:T(8,128)(2,1)}, u32[]{:S(2)}, u32[]{:S(2)}) collective-permute-start(bf16[2,128,1024]{2,1,0:T(8,128)(2,1)} %get-tuple-element.102), channel_id=1, source_target_pairs={{8,0},{16,8},{24,16},{28,24},{20,28},{12,20},{4,12},{0,4},{9,1},{1... | collective-permute-start | bytes 1572872 | tf_op jit(solution)/shard_map/ppermute | solution.py:144
  (51 other events, 633.1 us)
Sparse Core Ops, SparseCore 0:
  22.6 58.9 all-gather.1
  398.2 61.8 reduce-scatter.1
